TPU v7x, 32 devices: a whole 2x2x4 slice. The times are simulated.
32 devices in a mesh: sub: 16 (over z, y, core), row: 2 (over x).
Axes of the slice: x: 2, y: 2, z: 4, core: 2. Of those that a mesh axis runs over, the one named last changes fastest.
Arguments:
- compliance: bfloat16 [16, 36, 18, 128, 128], P('sub', 'row'), may hold values from -0.0625 to 0.0625
- block_columns: int32 [16, 36, 18], P('sub', 'row'), may hold values from 0 to 35, as said below
- load_response: bfloat16 [16, 32, 4608], P('sub', None, 'row'), may hold values from -6 to 6
- starting_motion: bfloat16 [16, 32, 4608], P('sub', None, 'row'), may hold values from -6 to 6
- start_traction: bfloat16 [16, 32, 4608], P('sub', None, 'row'), may hold values from -6 to 6
- stiffness: float32 [16, 4608], P('sub', 'row'), may hold values from 1 to 10
- history: float32 [16, 4608], P('sub', 'row'), may hold values from 0 to 0.6
- face_partner: int32 [16, 36], P('sub', 'row'), may hold values from -1 to 8, as said below
- orientation: int32 [16, 36, 128], P('sub', 'row'), may hold values from 0 to 127, as said below
Outputs:
- displacement: bfloat16 [16, 32, 4608], P('sub', None, 'row')
- traction: bfloat16 [16, 32, 4608], P('sub', None, 'row')
Inputs may be any that keep to these rules, and one draw needn't show every extreme that they name: `block_columns`: each block row names 18 distinct face columns. `face_partner`: an entry is -1 for a free face, else the position, within the facing group of the same run of the neighbouring substructure, of the matched face. Matches are mutual. Faces facing s+1 on the last substructure and faces facing s-1 on the first are free. In some run of some substructure all 9 faces facing s+1 are matched. `orientation`: each face's row is a permutation of 0 to 127; matched faces carry mutually inverse permutations.
All inputs are finite; a program needn't handle non-finite values.
Results may differ from a plain program's by a relative error of at most 0.0045.
The roundings to bfloat16 on the way count: a program that leaves them out, or rounds other values in their place, can miss the bound.
Values may be sent and summed in bfloat16 or wider, within the bound.
No kernel may reach another device: no remote copies, remote signals or barrier semaphores. Data moves between devices by JAX's collectives and lax.ppermute only.
A program may use at most 64 MiB of HBM per device.

v0:
```python
import functools

import jax
import jax.numpy as jnp
from jax import lax
from jax.experimental import pallas as pl
from jax.experimental.pallas import tpu as pltpu
from jax.sharding import PartitionSpec as P

ITERS = 3
SUBLANES = 8
VMEM_BYTES = 24 * 2**20

ONSET_JUMP = 0.15
FAILURE_JUMP = 1.5

VMEM = pl.BlockSpec(memory_space=pltpu.VMEM)
SMEM = pl.BlockSpec(memory_space=pltpu.SMEM)
HBM = pl.BlockSpec(memory_space=pltpu.HBM)


def position(group):
    near = group * (lax.axis_index("sub") % 2)
    return group - near, near, lax.axis_index("row")


def lanes_of(face, extent):
    return pl.ds(pl.multiple_of(face * extent, extent), extent)


def prepare(motion_hbm, stress_hbm, load_hbm, stiff_hbm, record_hbm, turn_hbm, columns_hbm, partner_hbm,
            robin0_ref, robin1_ref, half0_ref, half1_ref, load_ref, stiff_ref, record_ref, turn_ref, columns_ref, partner_ref,
            motion_ref, stress_ref, sems):
    pairs = (
        (motion_hbm, motion_ref), (stress_hbm, stress_ref), (load_hbm, load_ref), (stiff_hbm, stiff_ref),
        (record_hbm, record_ref), (turn_hbm, turn_ref), (columns_hbm, columns_ref), (partner_hbm, partner_ref),
    )
    copies = [pltpu.make_async_copy(source, target, sems.at[n]) for n, (source, target) in enumerate(pairs)]
    for copy in copies:
        copy.start()
    for copy in copies[:2]:
        copy.wait()
    group, _, extent = robin0_ref.shape
    starts = position(group)
    for side, (robin_ref, half_ref) in enumerate(((robin0_ref, half0_ref), (robin1_ref, half1_ref))):
        for index in range(group):
            lanes = lanes_of(starts[side] + index, extent)
            robin = stress_ref[:, lanes].astype(jnp.float32) + motion_ref[:, lanes].astype(jnp.float32)
            robin_ref[index] = robin
            half_ref[index] = robin.astype(jnp.bfloat16)
    for copy in copies[2:]:
        copy.wait()


def fetch(blocks_hbm, blocks_ref, sems):
    copies = [
        pltpu.make_async_copy(blocks_hbm.at[face], blocks_ref.at[face], sems.at[face])
        for face in range(blocks_hbm.shape[0])
    ]
    for copy in copies:
        copy.start()
    for copy in copies:
        copy.wait()


def block_products(parts):
    times, extent = parts[0][0][0].shape
    zero = jnp.zeros_like(parts[0][0][1])
    depth = max(len(part) for part in parts)
    parts = [part + [(part[0][0], zero)] * (depth - len(part)) for part in parts]
    values = jnp.concatenate([jnp.concatenate([v for v, _ in part], axis=1) for part in parts], axis=0)
    blocks = jnp.concatenate([jnp.concatenate([c for _, c in part], axis=1) for part in parts], axis=0)
    product = lax.dot_general(values, blocks, (((1,), (1,)), ((), ())), preferred_element_type=jnp.float32)
    return [
        product[p * times : (p + 1) * times, p * extent : (p + 1) * extent] for p in range(len(parts))
    ]


def linear_section(side, columns_ref, compliance_ref, own0_ref, own1_ref, other0_ref, other1_ref, robin_ref, load_ref,
                   stiff_ref, record_ref, out_ref, half_ref):
    group, rows, extent = out_ref.shape
    times = own0_ref.shape[1]
    faces, stored = compliance_ref.shape[:2]
    *starts, mine = position(group)
    first = starts[side]
    for run, refs in ((mine, (own0_ref, own1_ref)), (1 - mine, (other0_ref, other1_ref))):
        for start, ref in zip(starts, refs):
            half_ref[pl.ds(run * faces + start, group)] = ref[...]

    def entries(face, begin, end):
        return [(half_ref[columns_ref[face, 0, j]], compliance_ref[face, j]) for j in range(begin, end)]

    def finish(index, product):
        lanes = lanes_of(first + index, extent)
        response = product + load_ref[:, lanes].astype(jnp.float32)
        out_ref[index, :times] = robin_ref[index] - 2.0 * response
        if rows > times:
            out_ref[index, times : times + 1] = stiff_ref[:, lanes]
            out_ref[index, times + 1 : times + 2] = record_ref[:, lanes]
            out_ref[index, times + 2 :] = jnp.zeros_like(out_ref[index, times + 2 :])

    for index in range(0, group - 1, 2):
        pair = block_products([entries(first + index + k, 0, stored) for k in range(2)])
        for k in range(2):
            finish(index + k, pair[k])
    if group % 2:
        face = first + group - 1
        cut = (stored + 3) // 4 * 2
        finish(group - 1, sum(block_products([entries(face, 0, cut), entries(face, cut, stored)])))


def running_peak(sizes):
    row = lax.broadcasted_iota(jnp.int32, sizes.shape, 0)
    step = 1
    while step < sizes.shape[0]:
        earlier = pltpu.roll(sizes, step, 0)
        sizes = jnp.maximum(sizes, jnp.where(row >= step, earlier, 0.0))
        step *= 2
    return sizes


def local_face(times, ascent, mate, turn, stiffness, record, live, begin):
    extent = ascent.shape[1]
    gather = functools.partial(jnp.take_along_axis, axis=1, mode="promise_in_bounds")
    mate_ascent = gather(mate[:times], jnp.broadcast_to(turn, (times, extent)))
    if begin:
        constants = gather(mate[times:], jnp.broadcast_to(turn, (SUBLANES, extent)))
        stiffness = 0.5 * (stiffness + constants[:1])
        record = jnp.maximum(record, constants[1:2])
    difference = ascent - mate_ascent
    jump = difference / (1.0 + 2.0 * stiffness)
    peak = jnp.maximum(record, running_peak(jnp.abs(jump)))
    damage = jnp.clip((peak - ONSET_JUMP) / (FAILURE_JUMP - ONSET_JUMP), 0.0, 1.0)
    effective = stiffness * (1.0 - damage)
    traction = jnp.where(live, effective * difference / (1.0 + 2.0 * effective), 0.0)
    return traction, traction - ascent, stiffness, record


def local_group(side, begin, partner_ref, turn_ref, own_ref, mate_ref, stiff_ref, record_ref, robin_ref, half_ref, *pair_refs):
    group, times, extent = robin_ref.shape
    first = position(group)[side]
    for index in range(group):
        face = first + index
        partner = partner_ref[0, face]
        constants = lanes_of(face if begin else index, extent)
        traction, motion, stiffness, record = local_face(
            times, own_ref[index, :times], mate_ref[jnp.maximum(partner, 0)], turn_ref[:, lanes_of(face, extent)],
            stiff_ref[:, constants], record_ref[:, constants], partner >= 0, begin,
        )
        robin = traction + motion
        robin_ref[index] = robin
        half_ref[index] = robin.astype(jnp.bfloat16)
        if begin:
            pair_refs[0][:, lanes_of(index, extent)] = stiffness
            pair_refs[1][:, lanes_of(index, extent)] = record


def local_last(partner_ref, turn_ref, own0_ref, own1_ref, mate0_ref, mate1_ref, stiff0_ref, stiff1_ref,
               record0_ref, record1_ref, motion_ref, traction_ref):
    group, times, extent = own0_ref.shape
    starts = position(group)
    for side, (own_ref, mate_ref, stiff_ref, record_ref) in enumerate((
        (own0_ref, mate0_ref, stiff0_ref, record0_ref), (own1_ref, mate1_ref, stiff1_ref, record1_ref),
    )):
        for index in range(group):
            face = starts[side] + index
            lanes, constants = lanes_of(face, extent), lanes_of(index, extent)
            partner = partner_ref[0, face]
            traction, motion, _, _ = local_face(
                times, own_ref[index], mate_ref[jnp.maximum(partner, 0)], turn_ref[:, lanes],
                stiff_ref[:, constants], record_ref[:, constants], partner >= 0, False,
            )
            motion_ref[:, lanes] = motion.astype(jnp.bfloat16)
            traction_ref[:, lanes] = traction.astype(jnp.bfloat16)


def shards(
    compliance,
    block_columns,
    load_response,
    starting_motion,
    start_traction,
    stiffness,
    history,
    face_partner,
    orientation,
):
    _, faces, stored, extent, _ = compliance.shape
    times = starting_motion.shape[1]
    group = faces // 2
    subs = lax.axis_size("sub")
    rows = lax.axis_size("row")
    near_pairs = [(s, s ^ 1) for s in range(subs) if s ^ 1 < subs]
    far_pairs = [(s, t) for s in range(subs) for t in [s - 1 if s % 2 == 0 else s + 1] if 0 <= t < subs]
    swap = [(r, rows - 1 - r) for r in range(rows)]

    def f32(*shape):
        return jax.ShapeDtypeStruct(shape, jnp.float32)

    def bf16(*shape):
        return jax.ShapeDtypeStruct(shape, jnp.bfloat16)

    def s32(*shape):
        return jax.ShapeDtypeStruct(shape, jnp.int32)

    def call(kernel, in_specs, out_shape, scratch=(), moved=0, out_specs=()):
        outs = out_shape if isinstance(out_shape, tuple) else (out_shape,)
        out_specs = out_specs or (VMEM,) * len(outs)
        return pl.pallas_call(
            kernel,
            out_shape=out_shape,
            in_specs=in_specs,
            out_specs=out_specs if isinstance(out_shape, tuple) else out_specs[0],
            scratch_shapes=scratch,
            compiler_params=pltpu.CompilerParams(vmem_limit_bytes=VMEM_BYTES),
            cost_estimate=pl.CostEstimate(flops=moved, bytes_accessed=moved, transcendentals=0) if moved else None,
        )

    part = (group, times, extent)
    flat = (times, faces * extent)
    block_bytes = faces * stored * extent * extent * 2
    part_bytes = group * times * extent * 4
    robin0, robin1, half0, half1, load, stiff, record, turn, columns, partner = call(
        prepare, [HBM] * 8,
        (f32(*part), f32(*part), bf16(*part), bf16(*part), bf16(*flat), f32(1, faces * extent), f32(1, faces * extent),
         s32(1, faces * extent), pltpu.SMEM((faces, 1, stored), jnp.int32), pltpu.SMEM((1, faces), jnp.int32)),
        [pltpu.VMEM(flat, jnp.bfloat16), pltpu.VMEM(flat, jnp.bfloat16), pltpu.SemaphoreType.DMA((8,))],
        8 * part_bytes, (VMEM,) * 8 + (SMEM,) * 2,
    )(*(pltpu.with_memory_space_constraint(value, pltpu.HBM) for value in (
        starting_motion[0], start_traction[0], load_response[0], stiffness, history,
        orientation.reshape(1, -1), jnp.transpose(block_columns, (1, 0, 2)), face_partner,
    )))
    columns, partner = (pltpu.with_memory_space_constraint(table, pltpu.SMEM) for table in (columns, partner))
    blocks = call(
        fetch, [HBM], pltpu.VMEM((faces, stored, extent, extent), jnp.bfloat16),
        [pltpu.SemaphoreType.DMA((faces,))], block_bytes,
    )(pltpu.with_memory_space_constraint(compliance[0], pltpu.HBM))

    robin, half = [robin0, robin1], [half0, half1]
    stiffs, records = [stiff, stiff], [record, record]
    for iteration in range(ITERS):
        begin, last = iteration == 0, iteration == ITERS - 1
        other = [lax.ppermute(half[side], "row", swap) for side in range(2)]
        ascent, mates = [None, None], [None, None]
        for side, pairs in enumerate((far_pairs, near_pairs)):
            ascent[side] = call(
                functools.partial(linear_section, side),
                [SMEM] + [VMEM] * 9,
                f32(group, times + SUBLANES if begin else times, extent),
                [pltpu.VMEM((rows * faces, times, extent), jnp.bfloat16)],
                2 * block_bytes,
            )(columns, blocks, *half, *other, robin[side], load, stiff, record)
            mates[side] = lax.ppermute(ascent[side], "sub", pairs)
        if last:
            return tuple(out[None] for out in call(
                local_last, [SMEM] + [VMEM] * 9, (bf16(*flat),) * 2,
            )(partner, turn, *ascent, *mates, *stiffs, *records))
        for side in range(2):
            outs = (f32(*part), bf16(*part))
            if begin:
                outs += (f32(1, group * extent),) * 2
            robin[side], half[side], *pair = call(
                functools.partial(local_group, side, begin), [SMEM] + [VMEM] * 5, outs,
            )(partner, turn, ascent[side], mates[side], stiffs[side], records[side])
            if begin:
                stiffs[side], records[side] = pair


def solution(mesh):
    in_specs = (
        P("sub", "row", None, None, None),
        P("sub", "row", None),
        P("sub", None, "row"),
        P("sub", None, "row"),
        P("sub", None, "row"),
        P("sub", "row"),
        P("sub", "row"),
        P("sub", "row"),
        P("sub", "row", None),
    )
    out_specs = (P("sub", None, "row"), P("sub", None, "row"))
    return jax.shard_map(shards, mesh=mesh, in_specs=in_specs, out_specs=out_specs, check_vma=False)
```

profile of v0, /device:TPU:0, one launch (start us, length us, event | category | flops | bytes accessed | tf_op | source)
XLA Modules:
  0.0 51.2 jit_solution(12587587678558272912)
XLA Ops:
  0.6 1.1 %shard_map.104 = (f32[9,32,128]{2,1,0:T(8,128)S(1)}, f32[9,32,128]{2,1,0:T(8,128)S(1)}, bf16[9,32,128]{2,1,0:T(8,128)(2,1)S(1)}, bf16[9,32,128]{2,1,0:T(8,128)(2...) custom-call(bf16[32,2304]{1,0:T(8,128)(2,1)} %bitcast.9, ...), custom_call_target="tpu_custom_call" | custom-call | flops 1179648 | bytes 1179648 | tf_op jit(solution)/shard_map/pallas_call | solution.py:223
  1.8 3.0 %collective-permute-start = (bf16[9,32,128]{2,1,0:T(8,128)(2,1)S(1)}, bf16[9,32,128]{2,1,0:T(8,128)(2,1)S(1)}, u32[]{:S(2)}, u32[]{:S(2)}) collective-permute-start(bf16[9,32,128]{2,1,0:T(8,128)(2,1)S(1)} %get-tuple-element.29.own0_ref), channel_id=1, source_target_pairs={{0,1},{1,0},{2,3},{3,2},{4,5},{5,4},{6,7},{7,6},{8,9},{9,8},{10,11... | collective-permute-start | bytes 221192 | tf_op jit(solution)/shard_map/ppermute | solution.py:243
  4.8 0.1 collective-permute-start.1
  4.9 4.2 %shard_map.105.compliance_ref = bf16[18,18,128,128]{3,2,1,0:T(8,128)(2,1)S(1)} custom-call(bf16[18,18,128,128]{3,2,1,0:T(8,128)(2,1)} %bitcast.8), custom_call_target="tpu_custom_call" | custom-call | flops 10616832 | bytes 10616832 | tf_op jit(solution)/shard_map/pallas_call | solution.py:234
  9.1 0.1 collective-permute-done.1.other1_ref
  9.1 1.7 %shard_map.106.own_ref = f32[9,40,128]{2,1,0:T(8,128)S(1)} custom-call(s32[18,1,18]{2,1,0:T(1,128)S(4)} %get-tuple-element.28.columns_ref, bf16[18,18,128,128]{3,2,1,0:T(8,128)(2,1)S(1)} %shard_map.105.compliance_ref, bf16[9,32,128]{2,1,0:T(8,128)(2,1)S(1)} %get-tuple-element.29.own0_ref, bf16[9,32,128]{2,1,0:T(8,128)(2,1)S(1)} %get-tuple-element.30.own1_ref, ...), custom_call_target="tpu_custom_call" | custom-call | flops 21233664 | bytes 21233664 | tf_op jit(solution)/shard_map/pallas_call | solution.py:246
  10.9 0.7 %collective-permute-start.2 = (f32[9,40,128]{2,1,0:T(8,128)S(1)}, f32[9,40,128]{2,1,0:T(8,128)S(1)}, u32[]{:S(2)}, u32[]{:S(2)}) collective-permute-start(f32[9,40,128]{2,1,0:T(8,128)S(1)} %shard_map.106.own_ref), channel_id=1, source_target_pairs={{2,4},{4,2},{6,8},{8,6},{10,12},{12,10},{14,16},{16,14},{18,20},{2... | collective-permute-start | bytes 552968 | tf_op jit(solution)/shard_map/ppermute | solution.py:253
  11.6 1.7 %shard_map.108.own_ref = f32[9,40,128]{2,1,0:T(8,128)S(1)} custom-call(s32[18,1,18]{2,1,0:T(1,128)S(4)} %get-tuple-element.28.columns_ref, bf16[18,18,128,128]{3,2,1,0:T(8,128)(2,1)S(1)} %shard_map.105.compliance_ref, bf16[9,32,128]{2,1,0:T(8,128)(2,1)S(1)} %get-tuple-element.29.own0_ref, bf16[9,32,128]{2,1,0:T(8,128)(2,1)S(1)} %get-tuple-element.30.own1_ref, ...), custom_call_target="tpu_custom_call" | custom-call | flops 21233664 | bytes 21233664 | tf_op jit(solution)/shard_map/pallas_call | solution.py:246
  13.3 3.3 %collective-permute-start.3 = (f32[9,40,128]{2,1,0:T(8,128)S(1)}, f32[9,40,128]{2,1,0:T(8,128)S(1)}, u32[]{:S(2)}, u32[]{:S(2)}) collective-permute-start(f32[9,40,128]{2,1,0:T(8,128)S(1)} %shard_map.108.own_ref), channel_id=1, source_target_pairs={{0,2},{2,0},{4,6},{6,4},{8,10},{10,8},{12,14},{14,12},{16,18},{18,... | collective-permute-start | bytes 552968 | tf_op jit(solution)/shard_map/ppermute | solution.py:253
  16.7 0.3 shard_map.107
  16.9 1.6 %collective-permute-start.4 = (bf16[9,32,128]{2,1,0:T(8,128)(2,1)S(1)}, bf16[9,32,128]{2,1,0:T(8,128)(2,1)S(1)}, u32[]{:S(2)}, u32[]{:S(2)}) collective-permute-start(bf16[9,32,128]{2,1,0:T(8,128)(2,1)S(1)} %get-tuple-element.35.own0_ref), channel_id=1, source_target_pairs={{0,1},{1,0},{2,3},{3,2},{4,5},{5,4},{6,7},{7,6},{8,9},{9,8},{10,11... | collective-permute-start | bytes 221192 | tf_op jit(solution)/shard_map/ppermute | solution.py:243
  18.5 0.3 shard_map.109
  18.8 0.8 %collective-permute-start.5 = (bf16[9,32,128]{2,1,0:T(8,128)(2,1)S(1)}, bf16[9,32,128]{2,1,0:T(8,128)(2,1)S(1)}, u32[]{:S(2)}, u32[]{:S(2)}) collective-permute-start(bf16[9,32,128]{2,1,0:T(8,128)(2,1)S(1)} %get-tuple-element.37.own1_ref), channel_id=1, source_target_pairs={{0,1},{1,0},{2,3},{3,2},{4,5},{5,4},{6,7},{7,6},{8,9},{9,8},{10,11... | collective-permute-start | bytes 221192 | tf_op jit(solution)/shard_map/ppermute | solution.py:243
  19.5 1.8 %collective-permute-done.4.other0_ref = bf16[9,32,128]{2,1,0:T(8,128)(2,1)S(1)} collective-permute-done((bf16[9,32,128]{2,1,0:T(8,128)(2,1)S(1)}, bf16[9,32,128]{2,1,0:T(8,128)(2,1)S(1)}, u32[]{:S(2)}, u32[]{:S(2)}) %collective-permute-start.4) | collective-permute-done | bytes 73760 | tf_op jit(solution)/shard_map/ppermute | solution.py:243
  21.3 2.4 %collective-permute-done.5.other1_ref = bf16[9,32,128]{2,1,0:T(8,128)(2,1)S(1)} collective-permute-done((bf16[9,32,128]{2,1,0:T(8,128)(2,1)S(1)}, bf16[9,32,128]{2,1,0:T(8,128)(2,1)S(1)}, u32[]{:S(2)}, u32[]{:S(2)}) %collective-permute-start.5) | collective-permute-done | bytes 73760 | tf_op jit(solution)/shard_map/ppermute | solution.py:243
  23.8 1.7 %shard_map.110.own_ref = f32[9,32,128]{2,1,0:T(8,128)S(1)} custom-call(s32[18,1,18]{2,1,0:T(1,128)S(4)} %get-tuple-element.28.columns_ref, bf16[18,18,128,128]{3,2,1,0:T(8,128)(2,1)S(1)} %shard_map.105.compliance_ref, bf16[9,32,128]{2,1,0:T(8,128)(2,1)S(1)} %get-tuple-element.35.own0_ref, bf16[9,32,128]{2,1,0:T(8,128)(2,1)S(1)} %get-tuple-element.37.own1_ref, ...), custom_call_target="tpu_custom_call" | custom-call | flops 21233664 | bytes 21233664 | tf_op jit(solution)/shard_map/pallas_call | solution.py:246
  25.5 0.7 %collective-permute-start.6 = (f32[9,32,128]{2,1,0:T(8,128)S(1)}, f32[9,32,128]{2,1,0:T(8,128)S(1)}, u32[]{:S(2)}, u32[]{:S(2)}) collective-permute-start(f32[9,32,128]{2,1,0:T(8,128)S(1)} %shard_map.110.own_ref), channel_id=1, source_target_pairs={{2,4},{4,2},{6,8},{8,6},{10,12},{12,10},{14,16},{16,14},{18,20},{2... | collective-permute-start | bytes 442376 | tf_op jit(solution)/shard_map/ppermute | solution.py:253
  26.2 1.8 %shard_map.112.own_ref = f32[9,32,128]{2,1,0:T(8,128)S(1)} custom-call(s32[18,1,18]{2,1,0:T(1,128)S(4)} %get-tuple-element.28.columns_ref, bf16[18,18,128,128]{3,2,1,0:T(8,128)(2,1)S(1)} %shard_map.105.compliance_ref, bf16[9,32,128]{2,1,0:T(8,128)(2,1)S(1)} %get-tuple-element.35.own0_ref, bf16[9,32,128]{2,1,0:T(8,128)(2,1)S(1)} %get-tuple-element.37.own1_ref, ...), custom_call_target="tpu_custom_call" | custom-call | flops 21233664 | bytes 21233664 | tf_op jit(solution)/shard_map/pallas_call | solution.py:246
  27.9 5.8 %collective-permute-start.7 = (f32[9,32,128]{2,1,0:T(8,128)S(1)}, f32[9,32,128]{2,1,0:T(8,128)S(1)}, u32[]{:S(2)}, u32[]{:S(2)}) collective-permute-start(f32[9,32,128]{2,1,0:T(8,128)S(1)} %shard_map.112.own_ref), channel_id=1, source_target_pairs={{0,2},{2,0},{4,6},{6,4},{8,10},{10,8},{12,14},{14,12},{16,18},{18,... | collective-permute-start | bytes 442376 | tf_op jit(solution)/shard_map/ppermute | solution.py:253
  33.7 0.2 shard_map.111
  34.0 0.6 %collective-permute-start.8 = (bf16[9,32,128]{2,1,0:T(8,128)(2,1)S(1)}, bf16[9,32,128]{2,1,0:T(8,128)(2,1)S(1)}, u32[]{:S(2)}, u32[]{:S(2)}) collective-permute-start(bf16[9,32,128]{2,1,0:T(8,128)(2,1)S(1)} %get-tuple-element.41.own0_ref), channel_id=1, source_target_pairs={{0,1},{1,0},{2,3},{3,2},{4,5},{5,4},{6,7},{7,6},{8,9},{9,8},{10,11... | collective-permute-start | bytes 221192 | tf_op jit(solution)/shard_map/ppermute | solution.py:243
  34.6 0.1 collective-permute-done.7.mate_ref
  34.8 0.2 shard_map.113
  35.0 1.4 %collective-permute-start.9 = (bf16[9,32,128]{2,1,0:T(8,128)(2,1)S(1)}, bf16[9,32,128]{2,1,0:T(8,128)(2,1)S(1)}, u32[]{:S(2)}, u32[]{:S(2)}) collective-permute-start(bf16[9,32,128]{2,1,0:T(8,128)(2,1)S(1)} %get-tuple-element.45.own1_ref), channel_id=1, source_target_pairs={{0,1},{1,0},{2,3},{3,2},{4,5},{5,4},{6,7},{7,6},{8,9},{9,8},{10,11... | collective-permute-start | bytes 221192 | tf_op jit(solution)/shard_map/ppermute | solution.py:243
  36.4 2.5 %collective-permute-done.8.other0_ref = bf16[9,32,128]{2,1,0:T(8,128)(2,1)S(1)} collective-permute-done((bf16[9,32,128]{2,1,0:T(8,128)(2,1)S(1)}, bf16[9,32,128]{2,1,0:T(8,128)(2,1)S(1)}, u32[]{:S(2)}, u32[]{:S(2)}) %collective-permute-start.8) | collective-permute-done | bytes 73760 | tf_op jit(solution)/shard_map/ppermute | solution.py:243
  38.9 1.6 %collective-permute-done.9.other1_ref = bf16[9,32,128]{2,1,0:T(8,128)(2,1)S(1)} collective-permute-done((bf16[9,32,128]{2,1,0:T(8,128)(2,1)S(1)}, bf16[9,32,128]{2,1,0:T(8,128)(2,1)S(1)}, u32[]{:S(2)}, u32[]{:S(2)}) %collective-permute-start.9) | collective-permute-done | bytes 73760 | tf_op jit(solution)/shard_map/ppermute | solution.py:243
  40.5 1.7 %shard_map.114.own0_ref = f32[9,32,128]{2,1,0:T(8,128)S(1)} custom-call(s32[18,1,18]{2,1,0:T(1,128)S(4)} %get-tuple-element.28.columns_ref, bf16[18,18,128,128]{3,2,1,0:T(8,128)(2,1)S(1)} %shard_map.105.compliance_ref, bf16[9,32,128]{2,1,0:T(8,128)(2,1)S(1)} %get-tuple-element.41.own0_ref, bf16[9,32,128]{2,1,0:T(8,128)(2,1)S(1)} %get-tuple-element.45.own1_ref, ...), custom_call_target="tpu_custom_call" | custom-call | flops 21233664 | bytes 21233664 | tf_op jit(solution)/shard_map/pallas_call | solution.py:246
  42.2 0.7 %collective-permute-start.10 = (f32[9,32,128]{2,1,0:T(8,128)S(1)}, f32[9,32,128]{2,1,0:T(8,128)S(1)}, u32[]{:S(2)}, u32[]{:S(2)}) collective-permute-start(f32[9,32,128]{2,1,0:T(8,128)S(1)} %shard_map.114.own0_ref), channel_id=1, source_target_pairs={{2,4},{4,2},{6,8},{8,6},{10,12},{12,10},{14,16},{16,14},{18,20},{2... | collective-permute-start | bytes 442376 | tf_op jit(solution)/shard_map/ppermute | solution.py:253
  42.9 1.8 %shard_map.115.own1_ref = f32[9,32,128]{2,1,0:T(8,128)S(1)} custom-call(s32[18,1,18]{2,1,0:T(1,128)S(4)} %get-tuple-element.28.columns_ref, bf16[18,18,128,128]{3,2,1,0:T(8,128)(2,1)S(1)} %shard_map.105.compliance_ref, bf16[9,32,128]{2,1,0:T(8,128)(2,1)S(1)} %get-tuple-element.41.own0_ref, bf16[9,32,128]{2,1,0:T(8,128)(2,1)S(1)} %get-tuple-element.45.own1_ref, ...), custom_call_target="tpu_custom_call" | custom-call | flops 21233664 | bytes 21233664 | tf_op jit(solution)/shard_map/pallas_call | solution.py:246
  44.6 4.4 %collective-permute-start.11 = (f32[9,32,128]{2,1,0:T(8,128)S(1)}, f32[9,32,128]{2,1,0:T(8,128)S(1)}, u32[]{:S(2)}, u32[]{:S(2)}) collective-permute-start(f32[9,32,128]{2,1,0:T(8,128)S(1)} %shard_map.115.own1_ref), channel_id=1, source_target_pairs={{0,2},{2,0},{4,6},{6,4},{8,10},{10,8},{12,14},{14,12},{16,18},{18,... | collective-permute-start | bytes 442376 | tf_op jit(solution)/shard_map/ppermute | solution.py:253
  49.1 1.0 %collective-permute-done.11.mate1_ref = f32[9,32,128]{2,1,0:T(8,128)S(1)} collective-permute-done((f32[9,32,128]{2,1,0:T(8,128)S(1)}, f32[9,32,128]{2,1,0:T(8,128)S(1)}, u32[]{:S(2)}, u32[]{:S(2)}) %collective-permute-start.11) | collective-permute-done | bytes 147488 | tf_op jit(solution)/shard_map/ppermute | solution.py:253
  50.1 1.1 %shard_map.116 = (bf16[32,2304]{1,0:T(8,128)(2,1)}, bf16[32,2304]{1,0:T(8,128)(2,1)}) custom-call(s32[1,18]{1,0:T(1,128)S(4)} %get-tuple-element.26.partner_ref, s32[1,2304]{1,0:T(1,128)S(1)} %get-tuple-element.27.turn_ref, f32[9,32,128]{2,1,0:T(8,128)S(1)} %shard_map.114.own0_ref, f32[9,32,128]{2,1,0:T(8,128)S(1)} %shard_map.115.own1_ref, ...), custom_call_target="tpu_custom_call" | custom-call | tf_op jit(solution)/shard_map/pallas_call | solution.py:255
  (5 shorter events, 0.0 us)
Async XLA Ops:
  1.8 7.3 %collective-permute-start = (bf16[9,32,128]{2,1,0:T(8,128)(2,1)S(1)}, bf16[9,32,128]{2,1,0:T(8,128)(2,1)S(1)}, u32[]{:S(2)}, u32[]{:S(2)}) collective-permute-start(bf16[9,32,128]{2,1,0:T(8,128)(2,1)S(1)} %get-tuple-element.29.own0_ref), channel_id=1, source_target_pairs={{0,1},{1,0},{2,3},{3,2},{4,5},{5,4},{6,7},{7,6},{8,9},{9,8},{10,11... | collective-permute-start | bytes 221192 | tf_op jit(solution)/shard_map/ppermute | solution.py:243
  4.8 4.4 %collective-permute-start.1 = (bf16[9,32,128]{2,1,0:T(8,128)(2,1)S(1)}, bf16[9,32,128]{2,1,0:T(8,128)(2,1)S(1)}, u32[]{:S(2)}, u32[]{:S(2)}) collective-permute-start(bf16[9,32,128]{2,1,0:T(8,128)(2,1)S(1)} %get-tuple-element.30.own1_ref), channel_id=1, source_target_pairs={{0,1},{1,0},{2,3},{3,2},{4,5},{5,4},{6,7},{7,6},{8,9},{9,8},{10,11... | collective-permute-start | bytes 221192 | tf_op jit(solution)/shard_map/ppermute | solution.py:243
  10.9 5.8 %collective-permute-start.2 = (f32[9,40,128]{2,1,0:T(8,128)S(1)}, f32[9,40,128]{2,1,0:T(8,128)S(1)}, u32[]{:S(2)}, u32[]{:S(2)}) collective-permute-start(f32[9,40,128]{2,1,0:T(8,128)S(1)} %shard_map.106.own_ref), channel_id=1, source_target_pairs={{2,4},{4,2},{6,8},{8,6},{10,12},{12,10},{14,16},{16,14},{18,20},{2... | collective-permute-start | bytes 552968 | tf_op jit(solution)/shard_map/ppermute | solution.py:253
  13.3 5.2 %collective-permute-start.3 = (f32[9,40,128]{2,1,0:T(8,128)S(1)}, f32[9,40,128]{2,1,0:T(8,128)S(1)}, u32[]{:S(2)}, u32[]{:S(2)}) collective-permute-start(f32[9,40,128]{2,1,0:T(8,128)S(1)} %shard_map.108.own_ref), channel_id=1, source_target_pairs={{0,2},{2,0},{4,6},{6,4},{8,10},{10,8},{12,14},{14,12},{16,18},{18,... | collective-permute-start | bytes 552968 | tf_op jit(solution)/shard_map/ppermute | solution.py:253
  16.9 4.4 %collective-permute-start.4 = (bf16[9,32,128]{2,1,0:T(8,128)(2,1)S(1)}, bf16[9,32,128]{2,1,0:T(8,128)(2,1)S(1)}, u32[]{:S(2)}, u32[]{:S(2)}) collective-permute-start(bf16[9,32,128]{2,1,0:T(8,128)(2,1)S(1)} %get-tuple-element.35.own0_ref), channel_id=1, source_target_pairs={{0,1},{1,0},{2,3},{3,2},{4,5},{5,4},{6,7},{7,6},{8,9},{9,8},{10,11... | collective-permute-start | bytes 221192 | tf_op jit(solution)/shard_map/ppermute | solution.py:243
  18.8 5.0 %collective-permute-start.5 = (bf16[9,32,128]{2,1,0:T(8,128)(2,1)S(1)}, bf16[9,32,128]{2,1,0:T(8,128)(2,1)S(1)}, u32[]{:S(2)}, u32[]{:S(2)}) collective-permute-start(bf16[9,32,128]{2,1,0:T(8,128)(2,1)S(1)} %get-tuple-element.37.own1_ref), channel_id=1, source_target_pairs={{0,1},{1,0},{2,3},{3,2},{4,5},{5,4},{6,7},{7,6},{8,9},{9,8},{10,11... | collective-permute-start | bytes 221192 | tf_op jit(solution)/shard_map/ppermute | solution.py:243
  25.5 8.2 %collective-permute-start.6 = (f32[9,32,128]{2,1,0:T(8,128)S(1)}, f32[9,32,128]{2,1,0:T(8,128)S(1)}, u32[]{:S(2)}, u32[]{:S(2)}) collective-permute-start(f32[9,32,128]{2,1,0:T(8,128)S(1)} %shard_map.110.own_ref), channel_id=1, source_target_pairs={{2,4},{4,2},{6,8},{8,6},{10,12},{12,10},{14,16},{16,14},{18,20},{2... | collective-permute-start | bytes 442376 | tf_op jit(solution)/shard_map/ppermute | solution.py:253
  27.9 6.8 %collective-permute-start.7 = (f32[9,32,128]{2,1,0:T(8,128)S(1)}, f32[9,32,128]{2,1,0:T(8,128)S(1)}, u32[]{:S(2)}, u32[]{:S(2)}) collective-permute-start(f32[9,32,128]{2,1,0:T(8,128)S(1)} %shard_map.112.own_ref), channel_id=1, source_target_pairs={{0,2},{2,0},{4,6},{6,4},{8,10},{10,8},{12,14},{14,12},{16,18},{18,... | collective-permute-start | bytes 442376 | tf_op jit(solution)/shard_map/ppermute | solution.py:253
  34.0 4.9 %collective-permute-start.8 = (bf16[9,32,128]{2,1,0:T(8,128)(2,1)S(1)}, bf16[9,32,128]{2,1,0:T(8,128)(2,1)S(1)}, u32[]{:S(2)}, u32[]{:S(2)}) collective-permute-start(bf16[9,32,128]{2,1,0:T(8,128)(2,1)S(1)} %get-tuple-element.41.own0_ref), channel_id=1, source_target_pairs={{0,1},{1,0},{2,3},{3,2},{4,5},{5,4},{6,7},{7,6},{8,9},{9,8},{10,11... | collective-permute-start | bytes 221192 | tf_op jit(solution)/shard_map/ppermute | solution.py:243
  35.0 5.5 %collective-permute-start.9 = (bf16[9,32,128]{2,1,0:T(8,128)(2,1)S(1)}, bf16[9,32,128]{2,1,0:T(8,128)(2,1)S(1)}, u32[]{:S(2)}, u32[]{:S(2)}) collective-permute-start(bf16[9,32,128]{2,1,0:T(8,128)(2,1)S(1)} %get-tuple-element.45.own1_ref), channel_id=1, source_target_pairs={{0,1},{1,0},{2,3},{3,2},{4,5},{5,4},{6,7},{7,6},{8,9},{9,8},{10,11... | collective-permute-start | bytes 221192 | tf_op jit(solution)/shard_map/ppermute | solution.py:243
  42.2 6.9 %collective-permute-start.10 = (f32[9,32,128]{2,1,0:T(8,128)S(1)}, f32[9,32,128]{2,1,0:T(8,128)S(1)}, u32[]{:S(2)}, u32[]{:S(2)}) collective-permute-start(f32[9,32,128]{2,1,0:T(8,128)S(1)} %shard_map.114.own0_ref), channel_id=1, source_target_pairs={{2,4},{4,2},{6,8},{8,6},{10,12},{12,10},{14,16},{16,14},{18,20},{2... | collective-permute-start | bytes 442376 | tf_op jit(solution)/shard_map/ppermute | solution.py:253
  44.6 5.4 %collective-permute-start.11 = (f32[9,32,128]{2,1,0:T(8,128)S(1)}, f32[9,32,128]{2,1,0:T(8,128)S(1)}, u32[]{:S(2)}, u32[]{:S(2)}) collective-permute-start(f32[9,32,128]{2,1,0:T(8,128)S(1)} %shard_map.115.own1_ref), channel_id=1, source_target_pairs={{0,2},{2,0},{4,6},{6,4},{8,10},{10,8},{12,14},{14,12},{16,18},{18,... | collective-permute-start | bytes 442376 | tf_op jit(solution)/shard_map/ppermute | solution.py:253
where the time goes:
time: 52 us; the launch traced here: 51.2 us
  starting transfers between devices  23 us (44%)
  Pallas kernels  17.9 us (34%)
  waiting for transfers between devices  9.54 us (18%)
  between operations  0.76 us (1%)
    ppermute x6, starting transfers between devices, shards(): mates[side] = lax.ppermute(ascent[side], 'sub', pairs)  15.6 us
    pallas_call x6, Pallas kernels, shards(): call(functools.partial(linear_section, side), [SMEM] + [VMEM] * 9, f32(gr...  10.4 us
    ppermute x6, waiting for transfers between devices, shards(): other = [lax.ppermute(half[side], 'row', swap) for side in range(2)]  8.38 us
    ppermute x6, starting transfers between devices, shards(): other = [lax.ppermute(half[side], 'row', swap) for side in range(2)]  7.45 us
    pallas_call x1, Pallas kernels, shards(): call(fetch, [HBM], pltpu.VMEM((faces, stored, extent, extent), jnp.bfloat...  4.17 us
    ppermute x6, waiting for transfers between devices, shards(): mates[side] = lax.ppermute(ascent[side], 'sub', pairs)  1.16 us
    pallas_call x1, Pallas kernels, shards(): call(prepare, [HBM] * 8, (f32(*part), f32(*part), bf16(*part), bf16(*part...  1.15 us
    pallas_call x1, Pallas kernels, shards(): call(local_last, [SMEM] + [VMEM] * 9, (bf16(*flat),) * 2)  1.1 us
  transfers between devices with their start and end apart: 12, of which 7 were waited for; matrix products, arithmetic and copies ran while one was open for 0% of the time, Pallas kernels for 20%

commit v1 on v0

--- a/solution.py
+++ b/solution.py
@@ -21,7 +21,7 @@
 
 def position(group):
     near = group * (lax.axis_index("sub") % 2)
-    return group - near, near, lax.axis_index("row")
+    return near, group - near, lax.axis_index("row")
 
 
 def lanes_of(face, extent):
@@ -78,8 +78,8 @@
 
 def linear_section(side, columns_ref, compliance_ref, own0_ref, own1_ref, other0_ref, other1_ref, robin_ref, load_ref,
                    stiff_ref, record_ref, out_ref, half_ref):
-    group, rows, extent = out_ref.shape
-    times = own0_ref.shape[1]
+    group, times, extent = own0_ref.shape
+    rows = out_ref.shape[1]
     faces, stored = compliance_ref.shape[:2]
     *starts, mine = position(group)
     first = starts[side]
@@ -103,6 +103,8 @@
         pair = block_products([entries(first + index + k, 0, stored) for k in range(2)])
         for k in range(2):
             finish(index + k, pair[k])
+    for spare in range(group, out_ref.shape[0]):
+        out_ref[spare] = jnp.zeros_like(out_ref[spare])
     if group % 2:
         face = first + group - 1
         cut = (stored + 3) // 4 * 2
@@ -242,11 +244,11 @@
         begin, last = iteration == 0, iteration == ITERS - 1
         other = [lax.ppermute(half[side], "row", swap) for side in range(2)]
         ascent, mates = [None, None], [None, None]
-        for side, pairs in enumerate((far_pairs, near_pairs)):
+        for side, pairs in enumerate((near_pairs, far_pairs)):
             ascent[side] = call(
                 functools.partial(linear_section, side),
                 [SMEM] + [VMEM] * 9,
-                f32(group, times + SUBLANES if begin else times, extent),
+                f32(group + side, times + SUBLANES if begin else times, extent),
                 [pltpu.VMEM((rows * faces, times, extent), jnp.bfloat16)],
                 2 * block_bytes,
             )(columns, blocks, *half, *other, robin[side], load, stiff, record)

time: 52 us -> 50 us (0.962)
  starting transfers between devices: 23 us -> 19.6 us
  waiting for transfers between devices: 9.54 us -> 10.8 us
    ppermute x6, starting transfers between devices: 15.6 us -> 12.2 us  [shards(): mates[side] = lax.ppermute(ascent[side], 'sub', pairs)]
    ppermute x6, waiting for transfers between devices: 1.16 us -> 3.08 us  [shards(): mates[side] = lax.ppermute(ascent[side], 'sub', pairs)]
    ppermute x6, waiting for transfers between devices: 8.38 us -> 7.74 us  [shards(): other = [lax.ppermute(half[side], 'row', swap) for side in range(2)]]
  transfers between devices with their start and end apart: 12 -> 12, of which waited for: 7 -> 8; matrix products, arithmetic and copies ran while one was open for 0% -> 0% of each run, Pallas kernels for 20% -> 21%
where the time goes in v1:
time: 50 us; the launch traced here: 49 us
  starting transfers between devices  19.6 us (39%)
  Pallas kernels  17.8 us (36%)
  waiting for transfers between devices  10.8 us (22%)
  between operations  0.76 us (2%)
    ppermute x6, starting transfers between devices, shards(): mates[side] = lax.ppermute(ascent[side], 'sub', pairs)  12.2 us
    pallas_call x6, Pallas kernels, shards(): call(functools.partial(linear_section, side), [SMEM] + [VMEM] * 9, f32(gr...  10.4 us
    ppermute x6, waiting for transfers between devices, shards(): other = [lax.ppermute(half[side], 'row', swap) for side in range(2)]  7.74 us
    ppermute x6, starting transfers between devices, shards(): other = [lax.ppermute(half[side], 'row', swap) for side in range(2)]  7.42 us
    pallas_call x1, Pallas kernels, shards(): call(fetch, [HBM], pltpu.VMEM((faces, stored, extent, extent), jnp.bfloat...  4.17 us
    ppermute x6, waiting for transfers between devices, shards(): mates[side] = lax.ppermute(ascent[side], 'sub', pairs)  3.08 us
    pallas_call x1, Pallas kernels, shards(): call(prepare, [HBM] * 8, (f32(*part), f32(*part), bf16(*part), bf16(*part...  1.15 us
    pallas_call x1, Pallas kernels, shards(): call(local_last, [SMEM] + [VMEM] * 9, (bf16(*flat),) * 2)  1.11 us
  transfers between devices with their start and end apart: 12, of which 8 were waited for; matrix products, arithmetic and copies ran while one was open for 0% of the time, Pallas kernels for 21%

profile of v1, /device:TPU:0, one launch (start us, length us, event | category | flops | bytes accessed | tf_op | source)
XLA Modules:
  0.0 49.0 jit_solution(8825704008309723224)
XLA Ops:
  0.6 1.1 %shard_map.104 = (f32[9,32,128]{2,1,0:T(8,128)S(1)}, f32[9,32,128]{2,1,0:T(8,128)S(1)}, bf16[9,32,128]{2,1,0:T(8,128)(2,1)S(1)}, bf16[9,32,128]{2,1,0:T(8,128)(2...) custom-call(bf16[32,2304]{1,0:T(8,128)(2,1)} %bitcast.9, ...), custom_call_target="tpu_custom_call" | custom-call | flops 1179648 | bytes 1179648 | tf_op jit(solution)/shard_map/pallas_call | solution.py:225
  1.8 3.0 %collective-permute-start = (bf16[9,32,128]{2,1,0:T(8,128)(2,1)S(1)}, bf16[9,32,128]{2,1,0:T(8,128)(2,1)S(1)}, u32[]{:S(2)}, u32[]{:S(2)}) collective-permute-start(bf16[9,32,128]{2,1,0:T(8,128)(2,1)S(1)} %get-tuple-element.29.own0_ref), channel_id=1, source_target_pairs={{0,1},{1,0},{2,3},{3,2},{4,5},{5,4},{6,7},{7,6},{8,9},{9,8},{10,11... | collective-permute-start | bytes 221192 | tf_op jit(solution)/shard_map/ppermute | solution.py:245
  4.9 4.2 %shard_map.105.compliance_ref = bf16[18,18,128,128]{3,2,1,0:T(8,128)(2,1)S(1)} custom-call(bf16[18,18,128,128]{3,2,1,0:T(8,128)(2,1)} %bitcast.8), custom_call_target="tpu_custom_call" | custom-call | flops 10616832 | bytes 10616832 | tf_op jit(solution)/shard_map/pallas_call | solution.py:236
  9.1 0.1 collective-permute-done.1.other1_ref
  9.1 1.7 %shard_map.108.own_ref = f32[10,40,128]{2,1,0:T(8,128)S(1)} custom-call(s32[18,1,18]{2,1,0:T(1,128)S(4)} %get-tuple-element.28.columns_ref, bf16[18,18,128,128]{3,2,1,0:T(8,128)(2,1)S(1)} %shard_map.105.compliance_ref, bf16[9,32,128]{2,1,0:T(8,128)(2,1)S(1)} %get-tuple-element.29.own0_ref, bf16[9,32,128]{2,1,0:T(8,128)(2,1)S(1)} %get-tuple-element.30.own1_ref, ...), custom_call_target="tpu_custom_call" | custom-call | flops 21233664 | bytes 21233664 | tf_op jit(solution)/shard_map/pallas_call | solution.py:248
  10.9 0.7 %collective-permute-start.3 = (f32[10,40,128]{2,1,0:T(8,128)S(1)}, f32[10,40,128]{2,1,0:T(8,128)S(1)}, u32[]{:S(2)}, u32[]{:S(2)}) collective-permute-start(f32[10,40,128]{2,1,0:T(8,128)S(1)} %shard_map.108.own_ref), channel_id=1, source_target_pairs={{2,4},{4,2},{6,8},{8,6},{10,12},{12,10},{14,16},{16,14},{18,20},{2... | collective-permute-start | bytes 614408 | tf_op jit(solution)/shard_map/ppermute | solution.py:255
  11.6 1.7 %shard_map.106.own_ref = f32[9,40,128]{2,1,0:T(8,128)S(1)} custom-call(s32[18,1,18]{2,1,0:T(1,128)S(4)} %get-tuple-element.28.columns_ref, bf16[18,18,128,128]{3,2,1,0:T(8,128)(2,1)S(1)} %shard_map.105.compliance_ref, bf16[9,32,128]{2,1,0:T(8,128)(2,1)S(1)} %get-tuple-element.29.own0_ref, bf16[9,32,128]{2,1,0:T(8,128)(2,1)S(1)} %get-tuple-element.30.own1_ref, ...), custom_call_target="tpu_custom_call" | custom-call | flops 21233664 | bytes 21233664 | tf_op jit(solution)/shard_map/pallas_call | solution.py:248
  13.3 3.3 %collective-permute-start.2 = (f32[9,40,128]{2,1,0:T(8,128)S(1)}, f32[9,40,128]{2,1,0:T(8,128)S(1)}, u32[]{:S(2)}, u32[]{:S(2)}) collective-permute-start(f32[9,40,128]{2,1,0:T(8,128)S(1)} %shard_map.106.own_ref), channel_id=1, source_target_pairs={{0,2},{2,0},{4,6},{6,4},{8,10},{10,8},{12,14},{14,12},{16,18},{18,... | collective-permute-start | bytes 552968 | tf_op jit(solution)/shard_map/ppermute | solution.py:255
  16.6 1.1 %collective-permute-done.2.mate_ref = f32[9,40,128]{2,1,0:T(8,128)S(1)} collective-permute-done((f32[9,40,128]{2,1,0:T(8,128)S(1)}, f32[9,40,128]{2,1,0:T(8,128)S(1)}, u32[]{:S(2)}, u32[]{:S(2)}) %collective-permute-start.2) | collective-permute-done | bytes 184352 | tf_op jit(solution)/shard_map/ppermute | solution.py:255
  17.7 0.3 shard_map.107
  18.0 1.6 %collective-permute-start.4 = (bf16[9,32,128]{2,1,0:T(8,128)(2,1)S(1)}, bf16[9,32,128]{2,1,0:T(8,128)(2,1)S(1)}, u32[]{:S(2)}, u32[]{:S(2)}) collective-permute-start(bf16[9,32,128]{2,1,0:T(8,128)(2,1)S(1)} %get-tuple-element.35.own0_ref), channel_id=1, source_target_pairs={{0,1},{1,0},{2,3},{3,2},{4,5},{5,4},{6,7},{7,6},{8,9},{9,8},{10,11... | collective-permute-start | bytes 221192 | tf_op jit(solution)/shard_map/ppermute | solution.py:245
  19.5 0.3 shard_map.109
  19.8 0.6 %collective-permute-start.5 = (bf16[9,32,128]{2,1,0:T(8,128)(2,1)S(1)}, bf16[9,32,128]{2,1,0:T(8,128)(2,1)S(1)}, u32[]{:S(2)}, u32[]{:S(2)}) collective-permute-start(bf16[9,32,128]{2,1,0:T(8,128)(2,1)S(1)} %get-tuple-element.37.own1_ref), channel_id=1, source_target_pairs={{0,1},{1,0},{2,3},{3,2},{4,5},{5,4},{6,7},{7,6},{8,9},{9,8},{10,11... | collective-permute-start | bytes 221192 | tf_op jit(solution)/shard_map/ppermute | solution.py:245
  20.4 2.2 %collective-permute-done.4.other0_ref = bf16[9,32,128]{2,1,0:T(8,128)(2,1)S(1)} collective-permute-done((bf16[9,32,128]{2,1,0:T(8,128)(2,1)S(1)}, bf16[9,32,128]{2,1,0:T(8,128)(2,1)S(1)}, u32[]{:S(2)}, u32[]{:S(2)}) %collective-permute-start.4) | collective-permute-done | bytes 73760 | tf_op jit(solution)/shard_map/ppermute | solution.py:245
  22.6 1.7 %collective-permute-done.5.other1_ref = bf16[9,32,128]{2,1,0:T(8,128)(2,1)S(1)} collective-permute-done((bf16[9,32,128]{2,1,0:T(8,128)(2,1)S(1)}, bf16[9,32,128]{2,1,0:T(8,128)(2,1)S(1)}, u32[]{:S(2)}, u32[]{:S(2)}) %collective-permute-start.5) | collective-permute-done | bytes 73760 | tf_op jit(solution)/shard_map/ppermute | solution.py:245
  24.2 1.7 %shard_map.112.own_ref = f32[10,32,128]{2,1,0:T(8,128)S(1)} custom-call(s32[18,1,18]{2,1,0:T(1,128)S(4)} %get-tuple-element.28.columns_ref, bf16[18,18,128,128]{3,2,1,0:T(8,128)(2,1)S(1)} %shard_map.105.compliance_ref, bf16[9,32,128]{2,1,0:T(8,128)(2,1)S(1)} %get-tuple-element.35.own0_ref, bf16[9,32,128]{2,1,0:T(8,128)(2,1)S(1)} %get-tuple-element.37.own1_ref, ...), custom_call_target="tpu_custom_call" | custom-call | flops 21233664 | bytes 21233664 | tf_op jit(solution)/shard_map/pallas_call | solution.py:248
  26.0 0.7 %collective-permute-start.7 = (f32[10,32,128]{2,1,0:T(8,128)S(1)}, f32[10,32,128]{2,1,0:T(8,128)S(1)}, u32[]{:S(2)}, u32[]{:S(2)}) collective-permute-start(f32[10,32,128]{2,1,0:T(8,128)S(1)} %shard_map.112.own_ref), channel_id=1, source_target_pairs={{2,4},{4,2},{6,8},{8,6},{10,12},{12,10},{14,16},{16,14},{18,20},{2... | collective-permute-start | bytes 491528 | tf_op jit(solution)/shard_map/ppermute | solution.py:255
  26.6 1.7 %shard_map.110.own_ref = f32[9,32,128]{2,1,0:T(8,128)S(1)} custom-call(s32[18,1,18]{2,1,0:T(1,128)S(4)} %get-tuple-element.28.columns_ref, bf16[18,18,128,128]{3,2,1,0:T(8,128)(2,1)S(1)} %shard_map.105.compliance_ref, bf16[9,32,128]{2,1,0:T(8,128)(2,1)S(1)} %get-tuple-element.35.own0_ref, bf16[9,32,128]{2,1,0:T(8,128)(2,1)S(1)} %get-tuple-element.37.own1_ref, ...), custom_call_target="tpu_custom_call" | custom-call | flops 21233664 | bytes 21233664 | tf_op jit(solution)/shard_map/pallas_call | solution.py:248
  28.4 3.9 %collective-permute-start.6 = (f32[9,32,128]{2,1,0:T(8,128)S(1)}, f32[9,32,128]{2,1,0:T(8,128)S(1)}, u32[]{:S(2)}, u32[]{:S(2)}) collective-permute-start(f32[9,32,128]{2,1,0:T(8,128)S(1)} %shard_map.110.own_ref), channel_id=1, source_target_pairs={{0,2},{2,0},{4,6},{6,4},{8,10},{10,8},{12,14},{14,12},{16,18},{18,... | collective-permute-start | bytes 442376 | tf_op jit(solution)/shard_map/ppermute | solution.py:255
  32.3 1.0 %collective-permute-done.6.mate_ref = f32[9,32,128]{2,1,0:T(8,128)S(1)} collective-permute-done((f32[9,32,128]{2,1,0:T(8,128)S(1)}, f32[9,32,128]{2,1,0:T(8,128)S(1)}, u32[]{:S(2)}, u32[]{:S(2)}) %collective-permute-start.6) | collective-permute-done | bytes 147488 | tf_op jit(solution)/shard_map/ppermute | solution.py:255
  33.3 0.2 shard_map.111
  33.6 1.6 %collective-permute-start.8 = (bf16[9,32,128]{2,1,0:T(8,128)(2,1)S(1)}, bf16[9,32,128]{2,1,0:T(8,128)(2,1)S(1)}, u32[]{:S(2)}, u32[]{:S(2)}) collective-permute-start(bf16[9,32,128]{2,1,0:T(8,128)(2,1)S(1)} %get-tuple-element.41.own0_ref), channel_id=1, source_target_pairs={{0,1},{1,0},{2,3},{3,2},{4,5},{5,4},{6,7},{7,6},{8,9},{9,8},{10,11... | collective-permute-start | bytes 221192 | tf_op jit(solution)/shard_map/ppermute | solution.py:245
  35.2 0.2 shard_map.113
  35.4 0.6 %collective-permute-start.9 = (bf16[9,32,128]{2,1,0:T(8,128)(2,1)S(1)}, bf16[9,32,128]{2,1,0:T(8,128)(2,1)S(1)}, u32[]{:S(2)}, u32[]{:S(2)}) collective-permute-start(bf16[9,32,128]{2,1,0:T(8,128)(2,1)S(1)} %get-tuple-element.45.own1_ref), channel_id=1, source_target_pairs={{0,1},{1,0},{2,3},{3,2},{4,5},{5,4},{6,7},{7,6},{8,9},{9,8},{10,11... | collective-permute-start | bytes 221192 | tf_op jit(solution)/shard_map/ppermute | solution.py:245
  36.0 2.2 %collective-permute-done.8.other0_ref = bf16[9,32,128]{2,1,0:T(8,128)(2,1)S(1)} collective-permute-done((bf16[9,32,128]{2,1,0:T(8,128)(2,1)S(1)}, bf16[9,32,128]{2,1,0:T(8,128)(2,1)S(1)}, u32[]{:S(2)}, u32[]{:S(2)}) %collective-permute-start.8) | collective-permute-done | bytes 73760 | tf_op jit(solution)/shard_map/ppermute | solution.py:245
  38.2 1.6 %collective-permute-done.9.other1_ref = bf16[9,32,128]{2,1,0:T(8,128)(2,1)S(1)} collective-permute-done((bf16[9,32,128]{2,1,0:T(8,128)(2,1)S(1)}, bf16[9,32,128]{2,1,0:T(8,128)(2,1)S(1)}, u32[]{:S(2)}, u32[]{:S(2)}) %collective-permute-start.9) | collective-permute-done | bytes 73760 | tf_op jit(solution)/shard_map/ppermute | solution.py:245
  39.9 1.7 %shard_map.115.own1_ref = f32[10,32,128]{2,1,0:T(8,128)S(1)} custom-call(s32[18,1,18]{2,1,0:T(1,128)S(4)} %get-tuple-element.28.columns_ref, bf16[18,18,128,128]{3,2,1,0:T(8,128)(2,1)S(1)} %shard_map.105.compliance_ref, bf16[9,32,128]{2,1,0:T(8,128)(2,1)S(1)} %get-tuple-element.41.own0_ref, bf16[9,32,128]{2,1,0:T(8,128)(2,1)S(1)} %get-tuple-element.45.own1_ref, ...), custom_call_target="tpu_custom_call" | custom-call | flops 21233664 | bytes 21233664 | tf_op jit(solution)/shard_map/pallas_call | solution.py:248
  41.6 0.7 %collective-permute-start.11 = (f32[10,32,128]{2,1,0:T(8,128)S(1)}, f32[10,32,128]{2,1,0:T(8,128)S(1)}, u32[]{:S(2)}, u32[]{:S(2)}) collective-permute-start(f32[10,32,128]{2,1,0:T(8,128)S(1)} %shard_map.115.own1_ref), channel_id=1, source_target_pairs={{2,4},{4,2},{6,8},{8,6},{10,12},{12,10},{14,16},{16,14},{18,20},{2... | collective-permute-start | bytes 491528 | tf_op jit(solution)/shard_map/ppermute | solution.py:255
  42.3 1.7 %shard_map.114.own0_ref = f32[9,32,128]{2,1,0:T(8,128)S(1)} custom-call(s32[18,1,18]{2,1,0:T(1,128)S(4)} %get-tuple-element.28.columns_ref, bf16[18,18,128,128]{3,2,1,0:T(8,128)(2,1)S(1)} %shard_map.105.compliance_ref, bf16[9,32,128]{2,1,0:T(8,128)(2,1)S(1)} %get-tuple-element.41.own0_ref, bf16[9,32,128]{2,1,0:T(8,128)(2,1)S(1)} %get-tuple-element.45.own1_ref, ...), custom_call_target="tpu_custom_call" | custom-call | flops 21233664 | bytes 21233664 | tf_op jit(solution)/shard_map/pallas_call | solution.py:248
  44.0 2.9 %collective-permute-start.10 = (f32[9,32,128]{2,1,0:T(8,128)S(1)}, f32[9,32,128]{2,1,0:T(8,128)S(1)}, u32[]{:S(2)}, u32[]{:S(2)}) collective-permute-start(f32[9,32,128]{2,1,0:T(8,128)S(1)} %shard_map.114.own0_ref), channel_id=1, source_target_pairs={{0,2},{2,0},{4,6},{6,4},{8,10},{10,8},{12,14},{14,12},{16,18},{18,... | collective-permute-start | bytes 442376 | tf_op jit(solution)/shard_map/ppermute | solution.py:255
  46.9 1.0 %collective-permute-done.10.mate0_ref = f32[9,32,128]{2,1,0:T(8,128)S(1)} collective-permute-done((f32[9,32,128]{2,1,0:T(8,128)S(1)}, f32[9,32,128]{2,1,0:T(8,128)S(1)}, u32[]{:S(2)}, u32[]{:S(2)}) %collective-permute-start.10) | collective-permute-done | bytes 147488 | tf_op jit(solution)/shard_map/ppermute | solution.py:255
  47.9 1.1 %shard_map.116 = (bf16[32,2304]{1,0:T(8,128)(2,1)}, bf16[32,2304]{1,0:T(8,128)(2,1)}) custom-call(s32[1,18]{1,0:T(1,128)S(4)} %get-tuple-element.26.partner_ref, s32[1,2304]{1,0:T(1,128)S(1)} %get-tuple-element.27.turn_ref, f32[9,32,128]{2,1,0:T(8,128)S(1)} %shard_map.114.own0_ref, f32[10,32,128]{2,1,0:T(8,128)S(1)} %shard_map.115.own1_ref, ...), custom_call_target="tpu_custom_call" | custom-call | tf_op jit(solution)/shard_map/pallas_call | solution.py:257
  (5 shorter events, 0.1 us)
Async XLA Ops:
  1.8 7.3 %collective-permute-start = (bf16[9,32,128]{2,1,0:T(8,128)(2,1)S(1)}, bf16[9,32,128]{2,1,0:T(8,128)(2,1)S(1)}, u32[]{:S(2)}, u32[]{:S(2)}) collective-permute-start(bf16[9,32,128]{2,1,0:T(8,128)(2,1)S(1)} %get-tuple-element.29.own0_ref), channel_id=1, source_target_pairs={{0,1},{1,0},{2,3},{3,2},{4,5},{5,4},{6,7},{7,6},{8,9},{9,8},{10,11... | collective-permute-start | bytes 221192 | tf_op jit(solution)/shard_map/ppermute | solution.py:245
  4.8 4.4 %collective-permute-start.1 = (bf16[9,32,128]{2,1,0:T(8,128)(2,1)S(1)}, bf16[9,32,128]{2,1,0:T(8,128)(2,1)S(1)}, u32[]{:S(2)}, u32[]{:S(2)}) collective-permute-start(bf16[9,32,128]{2,1,0:T(8,128)(2,1)S(1)} %get-tuple-element.30.own1_ref), channel_id=1, source_target_pairs={{0,1},{1,0},{2,3},{3,2},{4,5},{5,4},{6,7},{7,6},{8,9},{9,8},{10,11... | collective-permute-start | bytes 221192 | tf_op jit(solution)/shard_map/ppermute | solution.py:245
  10.9 8.7 %collective-permute-start.3 = (f32[10,40,128]{2,1,0:T(8,128)S(1)}, f32[10,40,128]{2,1,0:T(8,128)S(1)}, u32[]{:S(2)}, u32[]{:S(2)}) collective-permute-start(f32[10,40,128]{2,1,0:T(8,128)S(1)} %shard_map.108.own_ref), channel_id=1, source_target_pairs={{2,4},{4,2},{6,8},{8,6},{10,12},{12,10},{14,16},{16,14},{18,20},{2... | collective-permute-start | bytes 614408 | tf_op jit(solution)/shard_map/ppermute | solution.py:255
  13.3 4.4 %collective-permute-start.2 = (f32[9,40,128]{2,1,0:T(8,128)S(1)}, f32[9,40,128]{2,1,0:T(8,128)S(1)}, u32[]{:S(2)}, u32[]{:S(2)}) collective-permute-start(f32[9,40,128]{2,1,0:T(8,128)S(1)} %shard_map.106.own_ref), channel_id=1, source_target_pairs={{0,2},{2,0},{4,6},{6,4},{8,10},{10,8},{12,14},{14,12},{16,18},{18,... | collective-permute-start | bytes 552968 | tf_op jit(solution)/shard_map/ppermute | solution.py:255
  18.0 4.6 %collective-permute-start.4 = (bf16[9,32,128]{2,1,0:T(8,128)(2,1)S(1)}, bf16[9,32,128]{2,1,0:T(8,128)(2,1)S(1)}, u32[]{:S(2)}, u32[]{:S(2)}) collective-permute-start(bf16[9,32,128]{2,1,0:T(8,128)(2,1)S(1)} %get-tuple-element.35.own0_ref), channel_id=1, source_target_pairs={{0,1},{1,0},{2,3},{3,2},{4,5},{5,4},{6,7},{7,6},{8,9},{9,8},{10,11... | collective-permute-start | bytes 221192 | tf_op jit(solution)/shard_map/ppermute | solution.py:245
  19.8 4.4 %collective-permute-start.5 = (bf16[9,32,128]{2,1,0:T(8,128)(2,1)S(1)}, bf16[9,32,128]{2,1,0:T(8,128)(2,1)S(1)}, u32[]{:S(2)}, u32[]{:S(2)}) collective-permute-start(bf16[9,32,128]{2,1,0:T(8,128)(2,1)S(1)} %get-tuple-element.37.own1_ref), channel_id=1, source_target_pairs={{0,1},{1,0},{2,3},{3,2},{4,5},{5,4},{6,7},{7,6},{8,9},{9,8},{10,11... | collective-permute-start | bytes 221192 | tf_op jit(solution)/shard_map/ppermute | solution.py:245
  26.0 9.2 %collective-permute-start.7 = (f32[10,32,128]{2,1,0:T(8,128)S(1)}, f32[10,32,128]{2,1,0:T(8,128)S(1)}, u32[]{:S(2)}, u32[]{:S(2)}) collective-permute-start(f32[10,32,128]{2,1,0:T(8,128)S(1)} %shard_map.112.own_ref), channel_id=1, source_target_pairs={{2,4},{4,2},{6,8},{8,6},{10,12},{12,10},{14,16},{16,14},{18,20},{2... | collective-permute-start | bytes 491528 | tf_op jit(solution)/shard_map/ppermute | solution.py:255
  28.4 5.0 %collective-permute-start.6 = (f32[9,32,128]{2,1,0:T(8,128)S(1)}, f32[9,32,128]{2,1,0:T(8,128)S(1)}, u32[]{:S(2)}, u32[]{:S(2)}) collective-permute-start(f32[9,32,128]{2,1,0:T(8,128)S(1)} %shard_map.110.own_ref), channel_id=1, source_target_pairs={{0,2},{2,0},{4,6},{6,4},{8,10},{10,8},{12,14},{14,12},{16,18},{18,... | collective-permute-start | bytes 442376 | tf_op jit(solution)/shard_map/ppermute | solution.py:255
  33.6 4.6 %collective-permute-start.8 = (bf16[9,32,128]{2,1,0:T(8,128)(2,1)S(1)}, bf16[9,32,128]{2,1,0:T(8,128)(2,1)S(1)}, u32[]{:S(2)}, u32[]{:S(2)}) collective-permute-start(bf16[9,32,128]{2,1,0:T(8,128)(2,1)S(1)} %get-tuple-element.41.own0_ref), channel_id=1, source_target_pairs={{0,1},{1,0},{2,3},{3,2},{4,5},{5,4},{6,7},{7,6},{8,9},{9,8},{10,11... | collective-permute-start | bytes 221192 | tf_op jit(solution)/shard_map/ppermute | solution.py:245
  35.4 4.4 %collective-permute-start.9 = (bf16[9,32,128]{2,1,0:T(8,128)(2,1)S(1)}, bf16[9,32,128]{2,1,0:T(8,128)(2,1)S(1)}, u32[]{:S(2)}, u32[]{:S(2)}) collective-permute-start(bf16[9,32,128]{2,1,0:T(8,128)(2,1)S(1)} %get-tuple-element.45.own1_ref), channel_id=1, source_target_pairs={{0,1},{1,0},{2,3},{3,2},{4,5},{5,4},{6,7},{7,6},{8,9},{9,8},{10,11... | collective-permute-start | bytes 221192 | tf_op jit(solution)/shard_map/ppermute | solution.py:245
  41.6 6.3 %collective-permute-start.11 = (f32[10,32,128]{2,1,0:T(8,128)S(1)}, f32[10,32,128]{2,1,0:T(8,128)S(1)}, u32[]{:S(2)}, u32[]{:S(2)}) collective-permute-start(f32[10,32,128]{2,1,0:T(8,128)S(1)} %shard_map.115.own1_ref), channel_id=1, source_target_pairs={{2,4},{4,2},{6,8},{8,6},{10,12},{12,10},{14,16},{16,14},{18,20},{2... | collective-permute-start | bytes 491528 | tf_op jit(solution)/shard_map/ppermute | solution.py:255
  44.0 3.9 %collective-permute-start.10 = (f32[9,32,128]{2,1,0:T(8,128)S(1)}, f32[9,32,128]{2,1,0:T(8,128)S(1)}, u32[]{:S(2)}, u32[]{:S(2)}) collective-permute-start(f32[9,32,128]{2,1,0:T(8,128)S(1)} %shard_map.114.own0_ref), channel_id=1, source_target_pairs={{0,2},{2,0},{4,6},{6,4},{8,10},{10,8},{12,14},{14,12},{16,18},{18,... | collective-permute-start | bytes 442376 | tf_op jit(solution)/shard_map/ppermute | solution.py:255

commit v2 on v1

--- a/solution.py
+++ b/solution.py
@@ -19,13 +19,12 @@
 HBM = pl.BlockSpec(memory_space=pltpu.HBM)
 
 
-def position(group):
-    near = group * (lax.axis_index("sub") % 2)
-    return near, group - near, lax.axis_index("row")
+def first_face(side, group):
+    return side * group
 
 
 def lanes_of(face, extent):
-    return pl.ds(pl.multiple_of(face * extent, extent), extent)
+    return slice(face * extent, (face + 1) * extent)
 
 
 def prepare(motion_hbm, stress_hbm, load_hbm, stiff_hbm, record_hbm, turn_hbm, columns_hbm, partner_hbm,
@@ -41,10 +40,9 @@
     for copy in copies[:2]:
         copy.wait()
     group, _, extent = robin0_ref.shape
-    starts = position(group)
     for side, (robin_ref, half_ref) in enumerate(((robin0_ref, half0_ref), (robin1_ref, half1_ref))):
         for index in range(group):
-            lanes = lanes_of(starts[side] + index, extent)
+            lanes = lanes_of(first_face(side, group) + index, extent)
             robin = stress_ref[:, lanes].astype(jnp.float32) + motion_ref[:, lanes].astype(jnp.float32)
             robin_ref[index] = robin
             half_ref[index] = robin.astype(jnp.bfloat16)
@@ -81,11 +79,11 @@
     group, times, extent = own0_ref.shape
     rows = out_ref.shape[1]
     faces, stored = compliance_ref.shape[:2]
-    *starts, mine = position(group)
-    first = starts[side]
+    first = first_face(side, group)
+    mine = lax.axis_index("row")
     for run, refs in ((mine, (own0_ref, own1_ref)), (1 - mine, (other0_ref, other1_ref))):
-        for start, ref in zip(starts, refs):
-            half_ref[pl.ds(run * faces + start, group)] = ref[...]
+        for part, ref in enumerate(refs):
+            half_ref[pl.ds(run * faces + first_face(part, group), group)] = ref[...]
 
     def entries(face, begin, end):
         return [(half_ref[columns_ref[face, 0, j]], compliance_ref[face, j]) for j in range(begin, end)]
@@ -103,8 +101,6 @@
         pair = block_products([entries(first + index + k, 0, stored) for k in range(2)])
         for k in range(2):
             finish(index + k, pair[k])
-    for spare in range(group, out_ref.shape[0]):
-        out_ref[spare] = jnp.zeros_like(out_ref[spare])
     if group % 2:
         face = first + group - 1
         cut = (stored + 3) // 4 * 2
@@ -140,7 +136,7 @@
 
 def local_group(side, begin, partner_ref, turn_ref, own_ref, mate_ref, stiff_ref, record_ref, robin_ref, half_ref, *pair_refs):
     group, times, extent = robin_ref.shape
-    first = position(group)[side]
+    first = first_face(side, group)
     for index in range(group):
         face = first + index
         partner = partner_ref[0, face]
@@ -160,12 +156,11 @@
 def local_last(partner_ref, turn_ref, own0_ref, own1_ref, mate0_ref, mate1_ref, stiff0_ref, stiff1_ref,
                record0_ref, record1_ref, motion_ref, traction_ref):
     group, times, extent = own0_ref.shape
-    starts = position(group)
     for side, (own_ref, mate_ref, stiff_ref, record_ref) in enumerate((
         (own0_ref, mate0_ref, stiff0_ref, record0_ref), (own1_ref, mate1_ref, stiff1_ref, record1_ref),
     )):
         for index in range(group):
-            face = starts[side] + index
+            face = first_face(side, group) + index
             lanes, constants = lanes_of(face, extent), lanes_of(index, extent)
             partner = partner_ref[0, face]
             traction, motion, _, _ = local_face(
@@ -192,8 +187,7 @@
     group = faces // 2
     subs = lax.axis_size("sub")
     rows = lax.axis_size("row")
-    near_pairs = [(s, s ^ 1) for s in range(subs) if s ^ 1 < subs]
-    far_pairs = [(s, t) for s in range(subs) for t in [s - 1 if s % 2 == 0 else s + 1] if 0 <= t < subs]
+    shifts = [[(s, (s + step) % subs) for s in range(subs)] for step in (1, -1)]
     swap = [(r, rows - 1 - r) for r in range(rows)]
 
     def f32(*shape):
@@ -244,20 +238,20 @@
         begin, last = iteration == 0, iteration == ITERS - 1
         other = [lax.ppermute(half[side], "row", swap) for side in range(2)]
         ascent, mates = [None, None], [None, None]
-        for side, pairs in enumerate((near_pairs, far_pairs)):
+        for side in range(2):
             ascent[side] = call(
                 functools.partial(linear_section, side),
                 [SMEM] + [VMEM] * 9,
-                f32(group + side, times + SUBLANES if begin else times, extent),
+                f32(group, times + SUBLANES if begin else times, extent),
                 [pltpu.VMEM((rows * faces, times, extent), jnp.bfloat16)],
                 2 * block_bytes,
             )(columns, blocks, *half, *other, robin[side], load, stiff, record)
-            mates[side] = lax.ppermute(ascent[side], "sub", pairs)
+            mates[1 - side] = lax.ppermute(ascent[side], "sub", shifts[side])
         if last:
             return tuple(out[None] for out in call(
                 local_last, [SMEM] + [VMEM] * 9, (bf16(*flat),) * 2,
             )(partner, turn, *ascent, *mates, *stiffs, *records))
-        for side in range(2):
+        for side in (1, 0):
             outs = (f32(*part), bf16(*part))
             if begin:
                 outs += (f32(1, group * extent),) * 2

time: 50 us -> 56.6 us (1.13); the launches traced: 49 us -> 56.4 us
  waiting for transfers between devices: 10.8 us -> 23.3 us
  starting transfers between devices: 19.6 us -> 14.5 us
    ppermute x6, waiting for transfers between devices: 3.08 us -> 17.5 us  [shards(): mates[1 - side] = lax.ppermute(ascent[side], 'sub', shifts[side])]
    ppermute x6, starting transfers between devices: 12.2 us -> 5.14 us  [shards(): mates[1 - side] = lax.ppermute(ascent[side], 'sub', shifts[side])]
    ppermute x6, waiting for transfers between devices: 7.74 us -> 5.8 us  [shards(): other = [lax.ppermute(half[side], 'row', swap) for side in range(2)]]
    ppermute x6, starting transfers between devices: 7.42 us -> 9.33 us  [shards(): other = [lax.ppermute(half[side], 'row', swap) for side in range(2)]]
  transfers between devices with their start and end apart: 12 -> 12, of which waited for: 8 -> 9; matrix products, arithmetic and copies ran while one was open for 0% -> 0% of each run, Pallas kernels for 21% -> 18%
where the time goes in v2:
time: 56.6 us; the launch traced here: 56.4 us
  waiting for transfers between devices  23.3 us (41%)
  Pallas kernels  17.8 us (31%)
  starting transfers between devices  14.5 us (26%)
  between operations  0.76 us (1%)
    ppermute x6, waiting for transfers between devices, shards(): mates[1 - side] = lax.ppermute(ascent[side], 'sub', shifts[side])  17.5 us
    pallas_call x6, Pallas kernels, shards(): call(functools.partial(linear_section, side), [SMEM] + [VMEM] * 9, f32(gr...  10.4 us
    ppermute x6, starting transfers between devices, shards(): other = [lax.ppermute(half[side], 'row', swap) for side in range(2)]  9.33 us
    ppermute x6, waiting for transfers between devices, shards(): other = [lax.ppermute(half[side], 'row', swap) for side in range(2)]  5.8 us
    ppermute x6, starting transfers between devices, shards(): mates[1 - side] = lax.ppermute(ascent[side], 'sub', shifts[side])  5.14 us
    pallas_call x1, Pallas kernels, shards(): call(fetch, [HBM], pltpu.VMEM((faces, stored, extent, extent), jnp.bfloat...  4.17 us
    pallas_call x1, Pallas kernels, shards(): call(prepare, [HBM] * 8, (f32(*part), f32(*part), bf16(*part), bf16(*part...  1.15 us
  transfers between devices with their start and end apart: 12, of which 9 were waited for; matrix products, arithmetic and copies ran while one was open for 0% of the time, Pallas kernels for 18%

profile of v2, /device:TPU:0, one launch (start us, length us, event | category | flops | bytes accessed | tf_op | source)
XLA Modules:
  0.0 56.4 jit_solution(9899921622502938361)
XLA Ops:
  0.6 1.1 %shard_map.104 = (f32[9,32,128]{2,1,0:T(8,128)S(1)}, f32[9,32,128]{2,1,0:T(8,128)S(1)}, bf16[9,32,128]{2,1,0:T(8,128)(2,1)S(1)}, bf16[9,32,128]{2,1,0:T(8,128)(2...) custom-call(bf16[32,2304]{1,0:T(8,128)(2,1)} %bitcast.9, ...), custom_call_target="tpu_custom_call" | custom-call | flops 1179648 | bytes 1179648 | tf_op jit(solution)/shard_map/pallas_call | solution.py:219
  1.8 3.0 %collective-permute-start = (bf16[9,32,128]{2,1,0:T(8,128)(2,1)S(1)}, bf16[9,32,128]{2,1,0:T(8,128)(2,1)S(1)}, u32[]{:S(2)}, u32[]{:S(2)}) collective-permute-start(bf16[9,32,128]{2,1,0:T(8,128)(2,1)S(1)} %get-tuple-element.29.own0_ref), channel_id=1, source_target_pairs={{0,1},{1,0},{2,3},{3,2},{4,5},{5,4},{6,7},{7,6},{8,9},{9,8},{10,11... | collective-permute-start | bytes 221192 | tf_op jit(solution)/shard_map/ppermute | solution.py:239
  4.8 0.1 collective-permute-start.1
  4.9 4.2 %shard_map.105.compliance_ref = bf16[18,18,128,128]{3,2,1,0:T(8,128)(2,1)S(1)} custom-call(bf16[18,18,128,128]{3,2,1,0:T(8,128)(2,1)} %bitcast.8), custom_call_target="tpu_custom_call" | custom-call | flops 10616832 | bytes 10616832 | tf_op jit(solution)/shard_map/pallas_call | solution.py:230
  9.1 0.1 collective-permute-done.1.other1_ref
  9.1 1.7 %shard_map.107.own_ref = f32[9,40,128]{2,1,0:T(8,128)S(1)} custom-call(s32[18,1,18]{2,1,0:T(1,128)S(4)} %get-tuple-element.28.columns_ref, bf16[18,18,128,128]{3,2,1,0:T(8,128)(2,1)S(1)} %shard_map.105.compliance_ref, bf16[9,32,128]{2,1,0:T(8,128)(2,1)S(1)} %get-tuple-element.29.own0_ref, bf16[9,32,128]{2,1,0:T(8,128)(2,1)S(1)} %get-tuple-element.30.own1_ref, ...), custom_call_target="tpu_custom_call" | custom-call | flops 21233664 | bytes 21233664 | tf_op jit(solution)/shard_map/pallas_call | solution.py:242
  10.9 3.9 %collective-permute-start.2 = (f32[9,40,128]{2,1,0:T(8,128)S(1)}, f32[9,40,128]{2,1,0:T(8,128)S(1)}, u32[]{:S(2)}, u32[]{:S(2)}) collective-permute-start(f32[9,40,128]{2,1,0:T(8,128)S(1)} %shard_map.107.own_ref), channel_id=1, source_target_pairs={{0,30},{2,0},{4,2},{6,4},{8,6},{10,8},{12,10},{14,12},{16,14},{18,... | collective-permute-start | bytes 552968 | tf_op jit(solution)/shard_map/ppermute | solution.py:249
  14.8 1.7 %shard_map.106.own_ref = f32[9,40,128]{2,1,0:T(8,128)S(1)} custom-call(s32[18,1,18]{2,1,0:T(1,128)S(4)} %get-tuple-element.28.columns_ref, bf16[18,18,128,128]{3,2,1,0:T(8,128)(2,1)S(1)} %shard_map.105.compliance_ref, bf16[9,32,128]{2,1,0:T(8,128)(2,1)S(1)} %get-tuple-element.29.own0_ref, bf16[9,32,128]{2,1,0:T(8,128)(2,1)S(1)} %get-tuple-element.30.own1_ref, ...), custom_call_target="tpu_custom_call" | custom-call | flops 21233664 | bytes 21233664 | tf_op jit(solution)/shard_map/pallas_call | solution.py:242
  16.6 1.3 %collective-permute-done.2.mate_ref = f32[9,40,128]{2,1,0:T(8,128)S(1)} collective-permute-done((f32[9,40,128]{2,1,0:T(8,128)S(1)}, f32[9,40,128]{2,1,0:T(8,128)S(1)}, u32[]{:S(2)}, u32[]{:S(2)}) %collective-permute-start.2) | collective-permute-done | bytes 184352 | tf_op jit(solution)/shard_map/ppermute | solution.py:249
  17.8 0.3 shard_map.108
  18.1 1.6 %collective-permute-start.4 = (bf16[9,32,128]{2,1,0:T(8,128)(2,1)S(1)}, bf16[9,32,128]{2,1,0:T(8,128)(2,1)S(1)}, u32[]{:S(2)}, u32[]{:S(2)}) collective-permute-start(bf16[9,32,128]{2,1,0:T(8,128)(2,1)S(1)} %get-tuple-element.36.own0_ref), channel_id=1, source_target_pairs={{0,1},{1,0},{2,3},{3,2},{4,5},{5,4},{6,7},{7,6},{8,9},{9,8},{10,11... | collective-permute-start | bytes 221192 | tf_op jit(solution)/shard_map/ppermute | solution.py:239
  19.6 4.6 %collective-permute-done.3.mate_ref = f32[9,40,128]{2,1,0:T(8,128)S(1)} collective-permute-done((f32[9,40,128]{2,1,0:T(8,128)S(1)}, f32[9,40,128]{2,1,0:T(8,128)S(1)}, u32[]{:S(2)}, u32[]{:S(2)}) %collective-permute-start.3) | collective-permute-done | bytes 184352 | tf_op jit(solution)/shard_map/ppermute | solution.py:249
  24.2 0.3 shard_map.109
  24.5 1.6 %collective-permute-start.5 = (bf16[9,32,128]{2,1,0:T(8,128)(2,1)S(1)}, bf16[9,32,128]{2,1,0:T(8,128)(2,1)S(1)}, u32[]{:S(2)}, u32[]{:S(2)}) collective-permute-start(bf16[9,32,128]{2,1,0:T(8,128)(2,1)S(1)} %get-tuple-element.37.own1_ref), channel_id=1, source_target_pairs={{0,1},{1,0},{2,3},{3,2},{4,5},{5,4},{6,7},{7,6},{8,9},{9,8},{10,11... | collective-permute-start | bytes 221192 | tf_op jit(solution)/shard_map/ppermute | solution.py:239
  26.0 2.9 %collective-permute-done.5.other1_ref = bf16[9,32,128]{2,1,0:T(8,128)(2,1)S(1)} collective-permute-done((bf16[9,32,128]{2,1,0:T(8,128)(2,1)S(1)}, bf16[9,32,128]{2,1,0:T(8,128)(2,1)S(1)}, u32[]{:S(2)}, u32[]{:S(2)}) %collective-permute-start.5) | collective-permute-done | bytes 73760 | tf_op jit(solution)/shard_map/ppermute | solution.py:239
  28.9 1.7 %shard_map.111.own_ref = f32[9,32,128]{2,1,0:T(8,128)S(1)} custom-call(s32[18,1,18]{2,1,0:T(1,128)S(4)} %get-tuple-element.28.columns_ref, bf16[18,18,128,128]{3,2,1,0:T(8,128)(2,1)S(1)} %shard_map.105.compliance_ref, bf16[9,32,128]{2,1,0:T(8,128)(2,1)S(1)} %get-tuple-element.36.own0_ref, bf16[9,32,128]{2,1,0:T(8,128)(2,1)S(1)} %get-tuple-element.37.own1_ref, ...), custom_call_target="tpu_custom_call" | custom-call | flops 21233664 | bytes 21233664 | tf_op jit(solution)/shard_map/pallas_call | solution.py:242
  30.7 1.7 %shard_map.110.own_ref = f32[9,32,128]{2,1,0:T(8,128)S(1)} custom-call(s32[18,1,18]{2,1,0:T(1,128)S(4)} %get-tuple-element.28.columns_ref, bf16[18,18,128,128]{3,2,1,0:T(8,128)(2,1)S(1)} %shard_map.105.compliance_ref, bf16[9,32,128]{2,1,0:T(8,128)(2,1)S(1)} %get-tuple-element.36.own0_ref, bf16[9,32,128]{2,1,0:T(8,128)(2,1)S(1)} %get-tuple-element.37.own1_ref, ...), custom_call_target="tpu_custom_call" | custom-call | flops 21233664 | bytes 21233664 | tf_op jit(solution)/shard_map/pallas_call | solution.py:242
  32.4 0.5 collective-permute-start.7
  33.0 0.4 collective-permute-done.6.mate_ref
  33.4 0.2 shard_map.112
  33.6 1.6 %collective-permute-start.8 = (bf16[9,32,128]{2,1,0:T(8,128)(2,1)S(1)}, bf16[9,32,128]{2,1,0:T(8,128)(2,1)S(1)}, u32[]{:S(2)}, u32[]{:S(2)}) collective-permute-start(bf16[9,32,128]{2,1,0:T(8,128)(2,1)S(1)} %get-tuple-element.42.own0_ref), channel_id=1, source_target_pairs={{0,1},{1,0},{2,3},{3,2},{4,5},{5,4},{6,7},{7,6},{8,9},{9,8},{10,11... | collective-permute-start | bytes 221192 | tf_op jit(solution)/shard_map/ppermute | solution.py:239
  35.2 4.6 %collective-permute-done.7.mate_ref = f32[9,32,128]{2,1,0:T(8,128)S(1)} collective-permute-done((f32[9,32,128]{2,1,0:T(8,128)S(1)}, f32[9,32,128]{2,1,0:T(8,128)S(1)}, u32[]{:S(2)}, u32[]{:S(2)}) %collective-permute-start.7) | collective-permute-done | bytes 147488 | tf_op jit(solution)/shard_map/ppermute | solution.py:249
  39.8 0.2 shard_map.113
  40.0 1.6 %collective-permute-start.9 = (bf16[9,32,128]{2,1,0:T(8,128)(2,1)S(1)}, bf16[9,32,128]{2,1,0:T(8,128)(2,1)S(1)}, u32[]{:S(2)}, u32[]{:S(2)}) collective-permute-start(bf16[9,32,128]{2,1,0:T(8,128)(2,1)S(1)} %get-tuple-element.45.own1_ref), channel_id=1, source_target_pairs={{0,1},{1,0},{2,3},{3,2},{4,5},{5,4},{6,7},{7,6},{8,9},{9,8},{10,11... | collective-permute-start | bytes 221192 | tf_op jit(solution)/shard_map/ppermute | solution.py:239
  41.6 2.9 %collective-permute-done.9.other1_ref = bf16[9,32,128]{2,1,0:T(8,128)(2,1)S(1)} collective-permute-done((bf16[9,32,128]{2,1,0:T(8,128)(2,1)S(1)}, bf16[9,32,128]{2,1,0:T(8,128)(2,1)S(1)}, u32[]{:S(2)}, u32[]{:S(2)}) %collective-permute-start.9) | collective-permute-done | bytes 73760 | tf_op jit(solution)/shard_map/ppermute | solution.py:239
  44.4 1.7 %shard_map.115.own1_ref = f32[9,32,128]{2,1,0:T(8,128)S(1)} custom-call(s32[18,1,18]{2,1,0:T(1,128)S(4)} %get-tuple-element.28.columns_ref, bf16[18,18,128,128]{3,2,1,0:T(8,128)(2,1)S(1)} %shard_map.105.compliance_ref, bf16[9,32,128]{2,1,0:T(8,128)(2,1)S(1)} %get-tuple-element.42.own0_ref, bf16[9,32,128]{2,1,0:T(8,128)(2,1)S(1)} %get-tuple-element.45.own1_ref, ...), custom_call_target="tpu_custom_call" | custom-call | flops 21233664 | bytes 21233664 | tf_op jit(solution)/shard_map/pallas_call | solution.py:242
  46.2 0.1 collective-permute-start.10
  46.2 1.7 %shard_map.114.own0_ref = f32[9,32,128]{2,1,0:T(8,128)S(1)} custom-call(s32[18,1,18]{2,1,0:T(1,128)S(4)} %get-tuple-element.28.columns_ref, bf16[18,18,128,128]{3,2,1,0:T(8,128)(2,1)S(1)} %shard_map.105.compliance_ref, bf16[9,32,128]{2,1,0:T(8,128)(2,1)S(1)} %get-tuple-element.42.own0_ref, bf16[9,32,128]{2,1,0:T(8,128)(2,1)S(1)} %get-tuple-element.45.own1_ref, ...), custom_call_target="tpu_custom_call" | custom-call | flops 21233664 | bytes 21233664 | tf_op jit(solution)/shard_map/pallas_call | solution.py:242
  48.0 0.5 collective-permute-start.11
  48.5 0.4 collective-permute-done.10.mate0_ref
  48.9 6.4 %collective-permute-done.11.mate1_ref = f32[9,32,128]{2,1,0:T(8,128)S(1)} collective-permute-done((f32[9,32,128]{2,1,0:T(8,128)S(1)}, f32[9,32,128]{2,1,0:T(8,128)S(1)}, u32[]{:S(2)}, u32[]{:S(2)}) %collective-permute-start.11) | collective-permute-done | bytes 147488 | tf_op jit(solution)/shard_map/ppermute | solution.py:249
  55.3 1.1 %shard_map.116 = (bf16[32,2304]{1,0:T(8,128)(2,1)}, bf16[32,2304]{1,0:T(8,128)(2,1)}) custom-call(s32[1,18]{1,0:T(1,128)S(4)} %get-tuple-element.26.partner_ref, s32[1,2304]{1,0:T(1,128)S(1)} %get-tuple-element.27.turn_ref, f32[9,32,128]{2,1,0:T(8,128)S(1)} %shard_map.114.own0_ref, f32[9,32,128]{2,1,0:T(8,128)S(1)} %shard_map.115.own1_ref, ...), custom_call_target="tpu_custom_call" | custom-call | tf_op jit(solution)/shard_map/pallas_call | solution.py:251
  (5 shorter events, 0.1 us)
Async XLA Ops:
  1.8 7.3 %collective-permute-start = (bf16[9,32,128]{2,1,0:T(8,128)(2,1)S(1)}, bf16[9,32,128]{2,1,0:T(8,128)(2,1)S(1)}, u32[]{:S(2)}, u32[]{:S(2)}) collective-permute-start(bf16[9,32,128]{2,1,0:T(8,128)(2,1)S(1)} %get-tuple-element.29.own0_ref), channel_id=1, source_target_pairs={{0,1},{1,0},{2,3},{3,2},{4,5},{5,4},{6,7},{7,6},{8,9},{9,8},{10,11... | collective-permute-start | bytes 221192 | tf_op jit(solution)/shard_map/ppermute | solution.py:239
  4.8 4.4 %collective-permute-start.1 = (bf16[9,32,128]{2,1,0:T(8,128)(2,1)S(1)}, bf16[9,32,128]{2,1,0:T(8,128)(2,1)S(1)}, u32[]{:S(2)}, u32[]{:S(2)}) collective-permute-start(bf16[9,32,128]{2,1,0:T(8,128)(2,1)S(1)} %get-tuple-element.30.own1_ref), channel_id=1, source_target_pairs={{0,1},{1,0},{2,3},{3,2},{4,5},{5,4},{6,7},{7,6},{8,9},{9,8},{10,11... | collective-permute-start | bytes 221192 | tf_op jit(solution)/shard_map/ppermute | solution.py:239
  10.9 6.9 %collective-permute-start.2 = (f32[9,40,128]{2,1,0:T(8,128)S(1)}, f32[9,40,128]{2,1,0:T(8,128)S(1)}, u32[]{:S(2)}, u32[]{:S(2)}) collective-permute-start(f32[9,40,128]{2,1,0:T(8,128)S(1)} %shard_map.107.own_ref), channel_id=1, source_target_pairs={{0,30},{2,0},{4,2},{6,4},{8,6},{10,8},{12,10},{14,12},{16,14},{18,... | collective-permute-start | bytes 552968 | tf_op jit(solution)/shard_map/ppermute | solution.py:249
  16.5 7.7 %collective-permute-start.3 = (f32[9,40,128]{2,1,0:T(8,128)S(1)}, f32[9,40,128]{2,1,0:T(8,128)S(1)}, u32[]{:S(2)}, u32[]{:S(2)}) collective-permute-start(f32[9,40,128]{2,1,0:T(8,128)S(1)} %shard_map.106.own_ref), channel_id=1, source_target_pairs={{0,2},{2,4},{4,6},{6,8},{8,10},{10,12},{12,14},{14,16},{16,18},{18... | collective-permute-start | bytes 552968 | tf_op jit(solution)/shard_map/ppermute | solution.py:249
  18.1 8.0 %collective-permute-start.4 = (bf16[9,32,128]{2,1,0:T(8,128)(2,1)S(1)}, bf16[9,32,128]{2,1,0:T(8,128)(2,1)S(1)}, u32[]{:S(2)}, u32[]{:S(2)}) collective-permute-start(bf16[9,32,128]{2,1,0:T(8,128)(2,1)S(1)} %get-tuple-element.36.own0_ref), channel_id=1, source_target_pairs={{0,1},{1,0},{2,3},{3,2},{4,5},{5,4},{6,7},{7,6},{8,9},{9,8},{10,11... | collective-permute-start | bytes 221192 | tf_op jit(solution)/shard_map/ppermute | solution.py:239
  24.5 4.4 %collective-permute-start.5 = (bf16[9,32,128]{2,1,0:T(8,128)(2,1)S(1)}, bf16[9,32,128]{2,1,0:T(8,128)(2,1)S(1)}, u32[]{:S(2)}, u32[]{:S(2)}) collective-permute-start(bf16[9,32,128]{2,1,0:T(8,128)(2,1)S(1)} %get-tuple-element.37.own1_ref), channel_id=1, source_target_pairs={{0,1},{1,0},{2,3},{3,2},{4,5},{5,4},{6,7},{7,6},{8,9},{9,8},{10,11... | collective-permute-start | bytes 221192 | tf_op jit(solution)/shard_map/ppermute | solution.py:239
  30.6 2.7 %collective-permute-start.6 = (f32[9,32,128]{2,1,0:T(8,128)S(1)}, f32[9,32,128]{2,1,0:T(8,128)S(1)}, u32[]{:S(2)}, u32[]{:S(2)}) collective-permute-start(f32[9,32,128]{2,1,0:T(8,128)S(1)} %shard_map.111.own_ref), channel_id=1, source_target_pairs={{0,30},{2,0},{4,2},{6,4},{8,6},{10,8},{12,10},{14,12},{16,14},{18,... | collective-permute-start | bytes 442376 | tf_op jit(solution)/shard_map/ppermute | solution.py:249
  32.4 7.3 %collective-permute-start.7 = (f32[9,32,128]{2,1,0:T(8,128)S(1)}, f32[9,32,128]{2,1,0:T(8,128)S(1)}, u32[]{:S(2)}, u32[]{:S(2)}) collective-permute-start(f32[9,32,128]{2,1,0:T(8,128)S(1)} %shard_map.110.own_ref), channel_id=1, source_target_pairs={{0,2},{2,4},{4,6},{6,8},{8,10},{10,12},{12,14},{14,16},{16,18},{18... | collective-permute-start | bytes 442376 | tf_op jit(solution)/shard_map/ppermute | solution.py:249
  33.6 8.0 %collective-permute-start.8 = (bf16[9,32,128]{2,1,0:T(8,128)(2,1)S(1)}, bf16[9,32,128]{2,1,0:T(8,128)(2,1)S(1)}, u32[]{:S(2)}, u32[]{:S(2)}) collective-permute-start(bf16[9,32,128]{2,1,0:T(8,128)(2,1)S(1)} %get-tuple-element.42.own0_ref), channel_id=1, source_target_pairs={{0,1},{1,0},{2,3},{3,2},{4,5},{5,4},{6,7},{7,6},{8,9},{9,8},{10,11... | collective-permute-start | bytes 221192 | tf_op jit(solution)/shard_map/ppermute | solution.py:239
  40.0 4.4 %collective-permute-start.9 = (bf16[9,32,128]{2,1,0:T(8,128)(2,1)S(1)}, bf16[9,32,128]{2,1,0:T(8,128)(2,1)S(1)}, u32[]{:S(2)}, u32[]{:S(2)}) collective-permute-start(bf16[9,32,128]{2,1,0:T(8,128)(2,1)S(1)} %get-tuple-element.45.own1_ref), channel_id=1, source_target_pairs={{0,1},{1,0},{2,3},{3,2},{4,5},{5,4},{6,7},{7,6},{8,9},{9,8},{10,11... | collective-permute-start | bytes 221192 | tf_op jit(solution)/shard_map/ppermute | solution.py:239
  46.2 2.7 %collective-permute-start.10 = (f32[9,32,128]{2,1,0:T(8,128)S(1)}, f32[9,32,128]{2,1,0:T(8,128)S(1)}, u32[]{:S(2)}, u32[]{:S(2)}) collective-permute-start(f32[9,32,128]{2,1,0:T(8,128)S(1)} %shard_map.115.own1_ref), channel_id=1, source_target_pairs={{0,30},{2,0},{4,2},{6,4},{8,6},{10,8},{12,10},{14,12},{16,14},{18,... | collective-permute-start | bytes 442376 | tf_op jit(solution)/shard_map/ppermute | solution.py:249
  48.0 7.3 %collective-permute-start.11 = (f32[9,32,128]{2,1,0:T(8,128)S(1)}, f32[9,32,128]{2,1,0:T(8,128)S(1)}, u32[]{:S(2)}, u32[]{:S(2)}) collective-permute-start(f32[9,32,128]{2,1,0:T(8,128)S(1)} %shard_map.114.own0_ref), channel_id=1, source_target_pairs={{0,2},{2,4},{4,6},{6,8},{8,10},{10,12},{12,14},{14,16},{16,18},{18... | collective-permute-start | bytes 442376 | tf_op jit(solution)/shard_map/ppermute | solution.py:249

commit v3 on v1

--- a/solution.py
+++ b/solution.py
@@ -192,8 +192,13 @@
     group = faces // 2
     subs = lax.axis_size("sub")
     rows = lax.axis_size("row")
-    near_pairs = [(s, s ^ 1) for s in range(subs) if s ^ 1 < subs]
-    far_pairs = [(s, t) for s in range(subs) for t in [s - 1 if s % 2 == 0 else s + 1] if 0 <= t < subs]
+    near_pairs = [(s, s ^ 1) for s in range(subs)]
+    far_pairs = []
+    for s in range(subs):
+        mate = s - 1 if s % 2 == 0 else s + 1
+        for r in range(rows):
+            there = mate * rows + r if 0 <= mate < subs else s * rows + rows - 1 - r
+            far_pairs.append((s * rows + r, there))
     swap = [(r, rows - 1 - r) for r in range(rows)]
 
     def f32(*shape):
@@ -244,7 +249,7 @@
         begin, last = iteration == 0, iteration == ITERS - 1
         other = [lax.ppermute(half[side], "row", swap) for side in range(2)]
         ascent, mates = [None, None], [None, None]
-        for side, pairs in enumerate((near_pairs, far_pairs)):
+        for side, (axes, pairs) in enumerate((("sub", near_pairs), (("sub", "row"), far_pairs))):
             ascent[side] = call(
                 functools.partial(linear_section, side),
                 [SMEM] + [VMEM] * 9,
@@ -252,7 +257,7 @@
                 [pltpu.VMEM((rows * faces, times, extent), jnp.bfloat16)],
                 2 * block_bytes,
             )(columns, blocks, *half, *other, robin[side], load, stiff, record)
-            mates[side] = lax.ppermute(ascent[side], "sub", pairs)
+            mates[side] = lax.ppermute(ascent[side], axes, pairs)
         if last:
             return tuple(out[None] for out in call(
                 local_last, [SMEM] + [VMEM] * 9, (bf16(*flat),) * 2,

time: 50 us -> 44.5 us (0.89); the launches traced: 49 us -> 44.4 us
  starting transfers between devices: 19.6 us -> 14.3 us
  waiting for transfers between devices: 10.8 us -> 11.5 us
    ppermute x6, starting transfers between devices: 12.2 us -> 6.74 us  [shards(): mates[side] = lax.ppermute(ascent[side], axes, pairs)]
    ppermute x6, waiting for transfers between devices: 3.08 us -> 4.15 us  [shards(): mates[side] = lax.ppermute(ascent[side], axes, pairs)]
  transfers between devices with their start and end apart: 12 -> 12, of which waited for: 8 -> 9; matrix products, arithmetic and copies ran while one was open for 0% -> 0% of each run, Pallas kernels for 21% -> 23%
where the time goes in v3:
time: 44.5 us; the launch traced here: 44.4 us
  Pallas kernels  17.8 us (40%)
  starting transfers between devices  14.3 us (32%)
  waiting for transfers between devices  11.5 us (26%)
  between operations  0.74 us (2%)
    pallas_call x6, Pallas kernels, shards(): call(functools.partial(linear_section, side), [SMEM] + [VMEM] * 9, f32(gr...  10.4 us
    ppermute x6, starting transfers between devices, shards(): other = [lax.ppermute(half[side], 'row', swap) for side in range(2)]  7.58 us
    ppermute x6, waiting for transfers between devices, shards(): other = [lax.ppermute(half[side], 'row', swap) for side in range(2)]  7.35 us
    ppermute x6, starting transfers between devices, shards(): mates[side] = lax.ppermute(ascent[side], axes, pairs)  6.74 us
    pallas_call x1, Pallas kernels, shards(): call(fetch, [HBM], pltpu.VMEM((faces, stored, extent, extent), jnp.bfloat...  4.17 us
    ppermute x6, waiting for transfers between devices, shards(): mates[side] = lax.ppermute(ascent[side], axes, pairs)  4.15 us
    pallas_call x1, Pallas kernels, shards(): call(prepare, [HBM] * 8, (f32(*part), f32(*part), bf16(*part), bf16(*part...  1.15 us
    pallas_call x1, Pallas kernels, shards(): call(local_last, [SMEM] + [VMEM] * 9, (bf16(*flat),) * 2)  1.11 us
  transfers between devices with their start and end apart: 12, of which 9 were waited for; matrix products, arithmetic and copies ran while one was open for 0% of the time, Pallas kernels for 23%

profile of v3, /device:TPU:0, one launch (start us, length us, event | category | flops | bytes accessed | tf_op | source)
XLA Modules:
  0.0 44.4 jit_solution(6185050965515544726)
XLA Ops:
  0.6 1.1 %shard_map.104 = (f32[9,32,128]{2,1,0:T(8,128)S(1)}, f32[9,32,128]{2,1,0:T(8,128)S(1)}, bf16[9,32,128]{2,1,0:T(8,128)(2,1)S(1)}, bf16[9,32,128]{2,1,0:T(8,128)(2...) custom-call(bf16[32,2304]{1,0:T(8,128)(2,1)} %bitcast.9, ...), custom_call_target="tpu_custom_call" | custom-call | flops 1179648 | bytes 1179648 | tf_op jit(solution)/shard_map/pallas_call | solution.py:230
  1.8 3.0 %collective-permute-start = (bf16[9,32,128]{2,1,0:T(8,128)(2,1)S(1)}, bf16[9,32,128]{2,1,0:T(8,128)(2,1)S(1)}, u32[]{:S(2)}, u32[]{:S(2)}) collective-permute-start(bf16[9,32,128]{2,1,0:T(8,128)(2,1)S(1)} %get-tuple-element.29.own0_ref), channel_id=1, source_target_pairs={{0,1},{1,0},{2,3},{3,2},{4,5},{5,4},{6,7},{7,6},{8,9},{9,8},{10,11... | collective-permute-start | bytes 221192 | tf_op jit(solution)/shard_map/ppermute | solution.py:250
  4.9 4.2 %shard_map.105.compliance_ref = bf16[18,18,128,128]{3,2,1,0:T(8,128)(2,1)S(1)} custom-call(bf16[18,18,128,128]{3,2,1,0:T(8,128)(2,1)} %bitcast.8), custom_call_target="tpu_custom_call" | custom-call | flops 10616832 | bytes 10616832 | tf_op jit(solution)/shard_map/pallas_call | solution.py:241
  9.1 1.7 %shard_map.108.own_ref = f32[10,40,128]{2,1,0:T(8,128)S(1)} custom-call(s32[18,1,18]{2,1,0:T(1,128)S(4)} %get-tuple-element.28.columns_ref, bf16[18,18,128,128]{3,2,1,0:T(8,128)(2,1)S(1)} %shard_map.105.compliance_ref, bf16[9,32,128]{2,1,0:T(8,128)(2,1)S(1)} %get-tuple-element.29.own0_ref, bf16[9,32,128]{2,1,0:T(8,128)(2,1)S(1)} %get-tuple-element.30.own1_ref, ...), custom_call_target="tpu_custom_call" | custom-call | flops 21233664 | bytes 21233664 | tf_op jit(solution)/shard_map/pallas_call | solution.py:253
  10.9 1.9 %collective-permute-start.3 = (f32[10,40,128]{2,1,0:T(8,128)S(1)}, f32[10,40,128]{2,1,0:T(8,128)S(1)}, u32[]{:S(2)}, u32[]{:S(2)}) collective-permute-start(f32[10,40,128]{2,1,0:T(8,128)S(1)} %shard_map.108.own_ref), channel_id=1, source_target_pairs={{0,1},{1,0},{2,4},{3,5},{4,2},{5,3},{6,8},{7,9},{8,6},{9,7},{10,12... | collective-permute-start | bytes 614408 | tf_op jit(solution)/shard_map/ppermute | solution.py:260
  12.8 1.7 %shard_map.106.own_ref = f32[9,40,128]{2,1,0:T(8,128)S(1)} custom-call(s32[18,1,18]{2,1,0:T(1,128)S(4)} %get-tuple-element.28.columns_ref, bf16[18,18,128,128]{3,2,1,0:T(8,128)(2,1)S(1)} %shard_map.105.compliance_ref, bf16[9,32,128]{2,1,0:T(8,128)(2,1)S(1)} %get-tuple-element.29.own0_ref, bf16[9,32,128]{2,1,0:T(8,128)(2,1)S(1)} %get-tuple-element.30.own1_ref, ...), custom_call_target="tpu_custom_call" | custom-call | flops 21233664 | bytes 21233664 | tf_op jit(solution)/shard_map/pallas_call | solution.py:253
  14.6 0.2 collective-permute-start.2
  14.8 1.3 %collective-permute-done.2.mate_ref = f32[9,40,128]{2,1,0:T(8,128)S(1)} collective-permute-done((f32[9,40,128]{2,1,0:T(8,128)S(1)}, f32[9,40,128]{2,1,0:T(8,128)S(1)}, u32[]{:S(2)}, u32[]{:S(2)}) %collective-permute-start.2) | collective-permute-done | bytes 184352 | tf_op jit(solution)/shard_map/ppermute | solution.py:260
  16.1 0.3 shard_map.107
  16.3 1.3 %collective-permute-start.4 = (bf16[9,32,128]{2,1,0:T(8,128)(2,1)S(1)}, bf16[9,32,128]{2,1,0:T(8,128)(2,1)S(1)}, u32[]{:S(2)}, u32[]{:S(2)}) collective-permute-start(bf16[9,32,128]{2,1,0:T(8,128)(2,1)S(1)} %get-tuple-element.35.own0_ref), channel_id=1, source_target_pairs={{0,1},{1,0},{2,3},{3,2},{4,5},{5,4},{6,7},{7,6},{8,9},{9,8},{10,11... | collective-permute-start | bytes 221192 | tf_op jit(solution)/shard_map/ppermute | solution.py:250
  17.7 0.3 shard_map.109
  17.9 1.0 %collective-permute-start.5 = (bf16[9,32,128]{2,1,0:T(8,128)(2,1)S(1)}, bf16[9,32,128]{2,1,0:T(8,128)(2,1)S(1)}, u32[]{:S(2)}, u32[]{:S(2)}) collective-permute-start(bf16[9,32,128]{2,1,0:T(8,128)(2,1)S(1)} %get-tuple-element.37.own1_ref), channel_id=1, source_target_pairs={{0,1},{1,0},{2,3},{3,2},{4,5},{5,4},{6,7},{7,6},{8,9},{9,8},{10,11... | collective-permute-start | bytes 221192 | tf_op jit(solution)/shard_map/ppermute | solution.py:250
  18.9 1.8 %collective-permute-done.4.other0_ref = bf16[9,32,128]{2,1,0:T(8,128)(2,1)S(1)} collective-permute-done((bf16[9,32,128]{2,1,0:T(8,128)(2,1)S(1)}, bf16[9,32,128]{2,1,0:T(8,128)(2,1)S(1)}, u32[]{:S(2)}, u32[]{:S(2)}) %collective-permute-start.4) | collective-permute-done | bytes 73760 | tf_op jit(solution)/shard_map/ppermute | solution.py:250
  20.7 1.6 %collective-permute-done.5.other1_ref = bf16[9,32,128]{2,1,0:T(8,128)(2,1)S(1)} collective-permute-done((bf16[9,32,128]{2,1,0:T(8,128)(2,1)S(1)}, bf16[9,32,128]{2,1,0:T(8,128)(2,1)S(1)}, u32[]{:S(2)}, u32[]{:S(2)}) %collective-permute-start.5) | collective-permute-done | bytes 73760 | tf_op jit(solution)/shard_map/ppermute | solution.py:250
  22.4 1.7 %shard_map.112.own_ref = f32[10,32,128]{2,1,0:T(8,128)S(1)} custom-call(s32[18,1,18]{2,1,0:T(1,128)S(4)} %get-tuple-element.28.columns_ref, bf16[18,18,128,128]{3,2,1,0:T(8,128)(2,1)S(1)} %shard_map.105.compliance_ref, bf16[9,32,128]{2,1,0:T(8,128)(2,1)S(1)} %get-tuple-element.35.own0_ref, bf16[9,32,128]{2,1,0:T(8,128)(2,1)S(1)} %get-tuple-element.37.own1_ref, ...), custom_call_target="tpu_custom_call" | custom-call | flops 21233664 | bytes 21233664 | tf_op jit(solution)/shard_map/pallas_call | solution.py:253
  24.1 1.5 %collective-permute-start.7 = (f32[10,32,128]{2,1,0:T(8,128)S(1)}, f32[10,32,128]{2,1,0:T(8,128)S(1)}, u32[]{:S(2)}, u32[]{:S(2)}) collective-permute-start(f32[10,32,128]{2,1,0:T(8,128)S(1)} %shard_map.112.own_ref), channel_id=1, source_target_pairs={{0,1},{1,0},{2,4},{3,5},{4,2},{5,3},{6,8},{7,9},{8,6},{9,7},{10,12... | collective-permute-start | bytes 491528 | tf_op jit(solution)/shard_map/ppermute | solution.py:260
  25.7 1.7 %shard_map.110.own_ref = f32[9,32,128]{2,1,0:T(8,128)S(1)} custom-call(s32[18,1,18]{2,1,0:T(1,128)S(4)} %get-tuple-element.28.columns_ref, bf16[18,18,128,128]{3,2,1,0:T(8,128)(2,1)S(1)} %shard_map.105.compliance_ref, bf16[9,32,128]{2,1,0:T(8,128)(2,1)S(1)} %get-tuple-element.35.own0_ref, bf16[9,32,128]{2,1,0:T(8,128)(2,1)S(1)} %get-tuple-element.37.own1_ref, ...), custom_call_target="tpu_custom_call" | custom-call | flops 21233664 | bytes 21233664 | tf_op jit(solution)/shard_map/pallas_call | solution.py:253
  27.4 1.2 %collective-permute-start.6 = (f32[9,32,128]{2,1,0:T(8,128)S(1)}, f32[9,32,128]{2,1,0:T(8,128)S(1)}, u32[]{:S(2)}, u32[]{:S(2)}) collective-permute-start(f32[9,32,128]{2,1,0:T(8,128)S(1)} %shard_map.110.own_ref), channel_id=1, source_target_pairs={{0,2},{2,0},{4,6},{6,4},{8,10},{10,8},{12,14},{14,12},{16,18},{18,... | collective-permute-start | bytes 442376 | tf_op jit(solution)/shard_map/ppermute | solution.py:260
  28.6 1.0 %collective-permute-done.6.mate_ref = f32[9,32,128]{2,1,0:T(8,128)S(1)} collective-permute-done((f32[9,32,128]{2,1,0:T(8,128)S(1)}, f32[9,32,128]{2,1,0:T(8,128)S(1)}, u32[]{:S(2)}, u32[]{:S(2)}) %collective-permute-start.6) | collective-permute-done | bytes 147488 | tf_op jit(solution)/shard_map/ppermute | solution.py:260
  29.6 0.2 shard_map.111
  29.9 1.6 %collective-permute-start.8 = (bf16[9,32,128]{2,1,0:T(8,128)(2,1)S(1)}, bf16[9,32,128]{2,1,0:T(8,128)(2,1)S(1)}, u32[]{:S(2)}, u32[]{:S(2)}) collective-permute-start(bf16[9,32,128]{2,1,0:T(8,128)(2,1)S(1)} %get-tuple-element.41.own0_ref), channel_id=1, source_target_pairs={{0,1},{1,0},{2,3},{3,2},{4,5},{5,4},{6,7},{7,6},{8,9},{9,8},{10,11... | collective-permute-start | bytes 221192 | tf_op jit(solution)/shard_map/ppermute | solution.py:250
  31.5 0.2 shard_map.113
  31.7 0.6 %collective-permute-start.9 = (bf16[9,32,128]{2,1,0:T(8,128)(2,1)S(1)}, bf16[9,32,128]{2,1,0:T(8,128)(2,1)S(1)}, u32[]{:S(2)}, u32[]{:S(2)}) collective-permute-start(bf16[9,32,128]{2,1,0:T(8,128)(2,1)S(1)} %get-tuple-element.45.own1_ref), channel_id=1, source_target_pairs={{0,1},{1,0},{2,3},{3,2},{4,5},{5,4},{6,7},{7,6},{8,9},{9,8},{10,11... | collective-permute-start | bytes 221192 | tf_op jit(solution)/shard_map/ppermute | solution.py:250
  32.3 2.2 %collective-permute-done.8.other0_ref = bf16[9,32,128]{2,1,0:T(8,128)(2,1)S(1)} collective-permute-done((bf16[9,32,128]{2,1,0:T(8,128)(2,1)S(1)}, bf16[9,32,128]{2,1,0:T(8,128)(2,1)S(1)}, u32[]{:S(2)}, u32[]{:S(2)}) %collective-permute-start.8) | collective-permute-done | bytes 73760 | tf_op jit(solution)/shard_map/ppermute | solution.py:250
  34.6 1.6 %collective-permute-done.9.other1_ref = bf16[9,32,128]{2,1,0:T(8,128)(2,1)S(1)} collective-permute-done((bf16[9,32,128]{2,1,0:T(8,128)(2,1)S(1)}, bf16[9,32,128]{2,1,0:T(8,128)(2,1)S(1)}, u32[]{:S(2)}, u32[]{:S(2)}) %collective-permute-start.9) | collective-permute-done | bytes 73760 | tf_op jit(solution)/shard_map/ppermute | solution.py:250
  36.1 1.7 %shard_map.115.own1_ref = f32[10,32,128]{2,1,0:T(8,128)S(1)} custom-call(s32[18,1,18]{2,1,0:T(1,128)S(4)} %get-tuple-element.28.columns_ref, bf16[18,18,128,128]{3,2,1,0:T(8,128)(2,1)S(1)} %shard_map.105.compliance_ref, bf16[9,32,128]{2,1,0:T(8,128)(2,1)S(1)} %get-tuple-element.41.own0_ref, bf16[9,32,128]{2,1,0:T(8,128)(2,1)S(1)} %get-tuple-element.45.own1_ref, ...), custom_call_target="tpu_custom_call" | custom-call | flops 21233664 | bytes 21233664 | tf_op jit(solution)/shard_map/pallas_call | solution.py:253
  37.9 1.5 %collective-permute-start.11 = (f32[10,32,128]{2,1,0:T(8,128)S(1)}, f32[10,32,128]{2,1,0:T(8,128)S(1)}, u32[]{:S(2)}, u32[]{:S(2)}) collective-permute-start(f32[10,32,128]{2,1,0:T(8,128)S(1)} %shard_map.115.own1_ref), channel_id=1, source_target_pairs={{0,1},{1,0},{2,4},{3,5},{4,2},{5,3},{6,8},{7,9},{8,6},{9,7},{10,12... | collective-permute-start | bytes 491528 | tf_op jit(solution)/shard_map/ppermute | solution.py:260
  39.4 1.7 %shard_map.114.own0_ref = f32[9,32,128]{2,1,0:T(8,128)S(1)} custom-call(s32[18,1,18]{2,1,0:T(1,128)S(4)} %get-tuple-element.28.columns_ref, bf16[18,18,128,128]{3,2,1,0:T(8,128)(2,1)S(1)} %shard_map.105.compliance_ref, bf16[9,32,128]{2,1,0:T(8,128)(2,1)S(1)} %get-tuple-element.41.own0_ref, bf16[9,32,128]{2,1,0:T(8,128)(2,1)S(1)} %get-tuple-element.45.own1_ref, ...), custom_call_target="tpu_custom_call" | custom-call | flops 21233664 | bytes 21233664 | tf_op jit(solution)/shard_map/pallas_call | solution.py:253
  41.1 0.3 collective-permute-start.10
  41.4 1.1 %collective-permute-done.10.mate0_ref = f32[9,32,128]{2,1,0:T(8,128)S(1)} collective-permute-done((f32[9,32,128]{2,1,0:T(8,128)S(1)}, f32[9,32,128]{2,1,0:T(8,128)S(1)}, u32[]{:S(2)}, u32[]{:S(2)}) %collective-permute-start.10) | collective-permute-done | bytes 147488 | tf_op jit(solution)/shard_map/ppermute | solution.py:260
  42.5 0.7 %collective-permute-done.11.mate1_ref = f32[10,32,128]{2,1,0:T(8,128)S(1)} collective-permute-done((f32[10,32,128]{2,1,0:T(8,128)S(1)}, f32[10,32,128]{2,1,0:T(8,128)S(1)}, u32[]{:S(2)}, u32[]{:S(2)}) %collective-permute-start.11) | collective-permute-done | bytes 163872 | tf_op jit(solution)/shard_map/ppermute | solution.py:260
  43.2 1.1 %shard_map.116 = (bf16[32,2304]{1,0:T(8,128)(2,1)}, bf16[32,2304]{1,0:T(8,128)(2,1)}) custom-call(s32[1,18]{1,0:T(1,128)S(4)} %get-tuple-element.26.partner_ref, s32[1,2304]{1,0:T(1,128)S(1)} %get-tuple-element.27.turn_ref, f32[9,32,128]{2,1,0:T(8,128)S(1)} %shard_map.114.own0_ref, f32[10,32,128]{2,1,0:T(8,128)S(1)} %shard_map.115.own1_ref, ...), custom_call_target="tpu_custom_call" | custom-call | tf_op jit(solution)/shard_map/pallas_call | solution.py:262
  (5 shorter events, 0.2 us)
Async XLA Ops:
  1.8 7.3 %collective-permute-start = (bf16[9,32,128]{2,1,0:T(8,128)(2,1)S(1)}, bf16[9,32,128]{2,1,0:T(8,128)(2,1)S(1)}, u32[]{:S(2)}, u32[]{:S(2)}) collective-permute-start(bf16[9,32,128]{2,1,0:T(8,128)(2,1)S(1)} %get-tuple-element.29.own0_ref), channel_id=1, source_target_pairs={{0,1},{1,0},{2,3},{3,2},{4,5},{5,4},{6,7},{7,6},{8,9},{9,8},{10,11... | collective-permute-start | bytes 221192 | tf_op jit(solution)/shard_map/ppermute | solution.py:250
  4.8 4.4 %collective-permute-start.1 = (bf16[9,32,128]{2,1,0:T(8,128)(2,1)S(1)}, bf16[9,32,128]{2,1,0:T(8,128)(2,1)S(1)}, u32[]{:S(2)}, u32[]{:S(2)}) collective-permute-start(bf16[9,32,128]{2,1,0:T(8,128)(2,1)S(1)} %get-tuple-element.30.own1_ref), channel_id=1, source_target_pairs={{0,1},{1,0},{2,3},{3,2},{4,5},{5,4},{6,7},{7,6},{8,9},{9,8},{10,11... | collective-permute-start | bytes 221192 | tf_op jit(solution)/shard_map/ppermute | solution.py:250
  10.9 6.8 %collective-permute-start.3 = (f32[10,40,128]{2,1,0:T(8,128)S(1)}, f32[10,40,128]{2,1,0:T(8,128)S(1)}, u32[]{:S(2)}, u32[]{:S(2)}) collective-permute-start(f32[10,40,128]{2,1,0:T(8,128)S(1)} %shard_map.108.own_ref), channel_id=1, source_target_pairs={{0,1},{1,0},{2,4},{3,5},{4,2},{5,3},{6,8},{7,9},{8,6},{9,7},{10,12... | collective-permute-start | bytes 614408 | tf_op jit(solution)/shard_map/ppermute | solution.py:260
  14.6 1.5 %collective-permute-start.2 = (f32[9,40,128]{2,1,0:T(8,128)S(1)}, f32[9,40,128]{2,1,0:T(8,128)S(1)}, u32[]{:S(2)}, u32[]{:S(2)}) collective-permute-start(f32[9,40,128]{2,1,0:T(8,128)S(1)} %shard_map.106.own_ref), channel_id=1, source_target_pairs={{0,2},{2,0},{4,6},{6,4},{8,10},{10,8},{12,14},{14,12},{16,18},{18,... | collective-permute-start | bytes 552968 | tf_op jit(solution)/shard_map/ppermute | solution.py:260
  16.3 4.4 %collective-permute-start.4 = (bf16[9,32,128]{2,1,0:T(8,128)(2,1)S(1)}, bf16[9,32,128]{2,1,0:T(8,128)(2,1)S(1)}, u32[]{:S(2)}, u32[]{:S(2)}) collective-permute-start(bf16[9,32,128]{2,1,0:T(8,128)(2,1)S(1)} %get-tuple-element.35.own0_ref), channel_id=1, source_target_pairs={{0,1},{1,0},{2,3},{3,2},{4,5},{5,4},{6,7},{7,6},{8,9},{9,8},{10,11... | collective-permute-start | bytes 221192 | tf_op jit(solution)/shard_map/ppermute | solution.py:250
  17.9 4.5 %collective-permute-start.5 = (bf16[9,32,128]{2,1,0:T(8,128)(2,1)S(1)}, bf16[9,32,128]{2,1,0:T(8,128)(2,1)S(1)}, u32[]{:S(2)}, u32[]{:S(2)}) collective-permute-start(bf16[9,32,128]{2,1,0:T(8,128)(2,1)S(1)} %get-tuple-element.37.own1_ref), channel_id=1, source_target_pairs={{0,1},{1,0},{2,3},{3,2},{4,5},{5,4},{6,7},{7,6},{8,9},{9,8},{10,11... | collective-permute-start | bytes 221192 | tf_op jit(solution)/shard_map/ppermute | solution.py:250
  24.1 7.3 %collective-permute-start.7 = (f32[10,32,128]{2,1,0:T(8,128)S(1)}, f32[10,32,128]{2,1,0:T(8,128)S(1)}, u32[]{:S(2)}, u32[]{:S(2)}) collective-permute-start(f32[10,32,128]{2,1,0:T(8,128)S(1)} %shard_map.112.own_ref), channel_id=1, source_target_pairs={{0,1},{1,0},{2,4},{3,5},{4,2},{5,3},{6,8},{7,9},{8,6},{9,7},{10,12... | collective-permute-start | bytes 491528 | tf_op jit(solution)/shard_map/ppermute | solution.py:260
  27.4 2.2 %collective-permute-start.6 = (f32[9,32,128]{2,1,0:T(8,128)S(1)}, f32[9,32,128]{2,1,0:T(8,128)S(1)}, u32[]{:S(2)}, u32[]{:S(2)}) collective-permute-start(f32[9,32,128]{2,1,0:T(8,128)S(1)} %shard_map.110.own_ref), channel_id=1, source_target_pairs={{0,2},{2,0},{4,6},{6,4},{8,10},{10,8},{12,14},{14,12},{16,18},{18,... | collective-permute-start | bytes 442376 | tf_op jit(solution)/shard_map/ppermute | solution.py:260
  29.9 4.7 %collective-permute-start.8 = (bf16[9,32,128]{2,1,0:T(8,128)(2,1)S(1)}, bf16[9,32,128]{2,1,0:T(8,128)(2,1)S(1)}, u32[]{:S(2)}, u32[]{:S(2)}) collective-permute-start(bf16[9,32,128]{2,1,0:T(8,128)(2,1)S(1)} %get-tuple-element.41.own0_ref), channel_id=1, source_target_pairs={{0,1},{1,0},{2,3},{3,2},{4,5},{5,4},{6,7},{7,6},{8,9},{9,8},{10,11... | collective-permute-start | bytes 221192 | tf_op jit(solution)/shard_map/ppermute | solution.py:250
  31.7 4.4 %collective-permute-start.9 = (bf16[9,32,128]{2,1,0:T(8,128)(2,1)S(1)}, bf16[9,32,128]{2,1,0:T(8,128)(2,1)S(1)}, u32[]{:S(2)}, u32[]{:S(2)}) collective-permute-start(bf16[9,32,128]{2,1,0:T(8,128)(2,1)S(1)} %get-tuple-element.45.own1_ref), channel_id=1, source_target_pairs={{0,1},{1,0},{2,3},{3,2},{4,5},{5,4},{6,7},{7,6},{8,9},{9,8},{10,11... | collective-permute-start | bytes 221192 | tf_op jit(solution)/shard_map/ppermute | solution.py:250
  37.9 5.4 %collective-permute-start.11 = (f32[10,32,128]{2,1,0:T(8,128)S(1)}, f32[10,32,128]{2,1,0:T(8,128)S(1)}, u32[]{:S(2)}, u32[]{:S(2)}) collective-permute-start(f32[10,32,128]{2,1,0:T(8,128)S(1)} %shard_map.115.own1_ref), channel_id=1, source_target_pairs={{0,1},{1,0},{2,4},{3,5},{4,2},{5,3},{6,8},{7,9},{8,6},{9,7},{10,12... | collective-permute-start | bytes 491528 | tf_op jit(solution)/shard_map/ppermute | solution.py:260
  41.1 1.4 %collective-permute-start.10 = (f32[9,32,128]{2,1,0:T(8,128)S(1)}, f32[9,32,128]{2,1,0:T(8,128)S(1)}, u32[]{:S(2)}, u32[]{:S(2)}) collective-permute-start(f32[9,32,128]{2,1,0:T(8,128)S(1)} %shard_map.114.own0_ref), channel_id=1, source_target_pairs={{0,2},{2,0},{4,6},{6,4},{8,10},{10,8},{12,14},{14,12},{16,18},{18,... | collective-permute-start | bytes 442376 | tf_op jit(solution)/shard_map/ppermute | solution.py:260

commit v4 on v3

--- a/solution.py
+++ b/solution.py
@@ -9,6 +9,7 @@
 
 ITERS = 3
 SUBLANES = 8
+EARLY = (6, 10)
 VMEM_BYTES = 24 * 2**20
 
 ONSET_JUMP = 0.15
@@ -16,6 +17,7 @@
 
 VMEM = pl.BlockSpec(memory_space=pltpu.VMEM)
 SMEM = pl.BlockSpec(memory_space=pltpu.SMEM)
+ANY = pl.BlockSpec(memory_space=pl.ANY)
 HBM = pl.BlockSpec(memory_space=pltpu.HBM)
 
 
@@ -28,17 +30,14 @@
     return pl.ds(pl.multiple_of(face * extent, extent), extent)
 
 
-def prepare(motion_hbm, stress_hbm, load_hbm, stiff_hbm, record_hbm, turn_hbm, columns_hbm, partner_hbm,
-            robin0_ref, robin1_ref, half0_ref, half1_ref, load_ref, stiff_ref, record_ref, turn_ref, columns_ref, partner_ref,
-            motion_ref, stress_ref, sems):
-    pairs = (
-        (motion_hbm, motion_ref), (stress_hbm, stress_ref), (load_hbm, load_ref), (stiff_hbm, stiff_ref),
-        (record_hbm, record_ref), (turn_hbm, turn_ref), (columns_hbm, columns_ref), (partner_hbm, partner_ref),
-    )
-    copies = [pltpu.make_async_copy(source, target, sems.at[n]) for n, (source, target) in enumerate(pairs)]
+def prepare(motion_hbm, stress_hbm, robin0_ref, robin1_ref, half0_ref, half1_ref, motion_ref, stress_ref, sems):
+    copies = [
+        pltpu.make_async_copy(motion_hbm, motion_ref, sems.at[0]),
+        pltpu.make_async_copy(stress_hbm, stress_ref, sems.at[1]),
+    ]
     for copy in copies:
         copy.start()
-    for copy in copies[:2]:
+    for copy in copies:
         copy.wait()
     group, _, extent = robin0_ref.shape
     starts = position(group)
@@ -48,18 +47,47 @@
             robin = stress_ref[:, lanes].astype(jnp.float32) + motion_ref[:, lanes].astype(jnp.float32)
             robin_ref[index] = robin
             half_ref[index] = robin.astype(jnp.bfloat16)
-    for copy in copies[2:]:
-        copy.wait()
-
-
-def fetch(blocks_hbm, blocks_ref, sems):
-    copies = [
-        pltpu.make_async_copy(blocks_hbm.at[face], blocks_ref.at[face], sems.at[face])
-        for face in range(blocks_hbm.shape[0])
+
+
+def sort_blocks(columns_ref, order_ref, sorted_ref, ready_ref):
+    faces, _, stored = columns_ref.shape
+    group = faces // 2
+    near, far, mine = position(group)
+    own = mine * faces
+    partner = (1 - mine) * faces + near
+
+    def sort_row(face, _):
+        in_far = (face >= far) & (face < far + group)
+        width = jnp.where(in_far, group, 0)
+        front, back = jnp.int32(0), jnp.int32(stored - 1)
+        for j in range(stored):
+            column = columns_ref[face, 0, j]
+            early = ((column >= own) & (column < own + faces)) | ((column >= partner) & (column < partner + width))
+            place = jnp.where(early, front, back)
+            order_ref[face, 0, place] = j
+            sorted_ref[face, 0, place] = column
+            front = jnp.where(early, front + 1, front)
+            back = jnp.where(early, back, back - 1)
+        ready_ref[0, face] = front
+        return 0
+
+    lax.fori_loop(0, faces, sort_row, 0)
+
+
+def fetch(blocks_hbm, load_hbm, stiff_hbm, record_hbm, turn_hbm, columns_hbm, partner_hbm,
+          blocks_ref, load_ref, stiff_ref, record_ref, turn_ref, partner_ref, order_ref, sorted_ref, ready_ref,
+          columns_ref, sems):
+    pairs = [
+        (columns_hbm, columns_ref), (load_hbm, load_ref), (stiff_hbm, stiff_ref), (record_hbm, record_ref),
+        (turn_hbm, turn_ref), (partner_hbm, partner_ref),
     ]
+    pairs += [(blocks_hbm.at[face], blocks_ref.at[face]) for face in range(blocks_hbm.shape[0])]
+    copies = [pltpu.make_async_copy(source, target, sems.at[n]) for n, (source, target) in enumerate(pairs)]
     for copy in copies:
         copy.start()
-    for copy in copies:
+    copies[0].wait()
+    sort_blocks(columns_ref, order_ref, sorted_ref, ready_ref)
+    for copy in copies[1:]:
         copy.wait()
 
 
@@ -76,39 +104,89 @@
     ]
 
 
-def linear_section(side, columns_ref, compliance_ref, own0_ref, own1_ref, other0_ref, other1_ref, robin_ref, load_ref,
-                   stiff_ref, record_ref, out_ref, half_ref):
+def group_products(first, group, entries, finish):
+    for index in range(0, group - 1, 2):
+        pair = block_products([entries(first + index + k) for k in range(2)])
+        for k in range(2):
+            finish(index + k, pair[k])
+    if group % 2:
+        whole = entries(first + group - 1)
+        cut = (len(whole) + 3) // 4 * 2
+        finish(group - 1, sum(block_products([whole[:cut], whole[cut:]])))
+
+
+def early_products(side, order_ref, sorted_ref, ready_ref, compliance_ref, own0_ref, own1_ref, *refs):
+    out_ref, half_ref = refs[-2:]
+    group, times, _ = out_ref.shape
+    faces = compliance_ref.shape[0]
+    *starts, mine = position(group)
+    none = half_ref.shape[0] - 1
+    half_ref[none] = jnp.zeros_like(half_ref[none])
+    for start, ref in zip(starts, (own0_ref, own1_ref)):
+        half_ref[pl.ds(mine * faces + start, group)] = ref[...]
+    for ref in refs[:side]:
+        half_ref[pl.ds((1 - mine) * faces + starts[0], group)] = ref[...]
+
+    def entries(face):
+        ready = ready_ref[0, face]
+        return [
+            (half_ref[jnp.where(slot < ready, sorted_ref[face, 0, slot], none)], compliance_ref[face, order_ref[face, 0, slot]])
+            for slot in range(EARLY[side])
+        ]
+
+    def finish(index, product):
+        out_ref[index] = product
+
+    group_products(starts[side], group, entries, finish)
+
+
+def linear_section(side, begin, order_ref, sorted_ref, ready_ref, compliance_ref, own0_ref, own1_ref, other0_ref, other1_ref,
+                   robin_ref, load_ref, *refs):
+    out_ref, half_ref = refs[-2:]
     group, times, extent = own0_ref.shape
     rows = out_ref.shape[1]
     faces, stored = compliance_ref.shape[:2]
     *starts, mine = position(group)
     first = starts[side]
-    for run, refs in ((mine, (own0_ref, own1_ref)), (1 - mine, (other0_ref, other1_ref))):
-        for start, ref in zip(starts, refs):
+    done = 0 if begin else EARLY[side]
+    for run, parts in ((mine, (own0_ref, own1_ref)), (1 - mine, (other0_ref, other1_ref))):
+        for start, ref in zip(starts, parts):
             half_ref[pl.ds(run * faces + start, group)] = ref[...]
 
-    def entries(face, begin, end):
-        return [(half_ref[columns_ref[face, 0, j]], compliance_ref[face, j]) for j in range(begin, end)]
+    def entry(face, slot):
+        return half_ref[sorted_ref[face, 0, slot]], compliance_ref[face, order_ref[face, 0, slot]]
+
+    def entries(face):
+        return [entry(face, slot) for slot in range(done, stored)]
 
     def finish(index, product):
         lanes = lanes_of(first + index, extent)
         response = product + load_ref[:, lanes].astype(jnp.float32)
+        if done:
+            response = response + refs[0][index]
         out_ref[index, :times] = robin_ref[index] - 2.0 * response
-        if rows > times:
-            out_ref[index, times : times + 1] = stiff_ref[:, lanes]
-            out_ref[index, times + 1 : times + 2] = record_ref[:, lanes]
+        if begin:
+            out_ref[index, times : times + 1] = refs[0][:, lanes]
+            out_ref[index, times + 1 : times + 2] = refs[1][:, lanes]
             out_ref[index, times + 2 :] = jnp.zeros_like(out_ref[index, times + 2 :])
 
-    for index in range(0, group - 1, 2):
-        pair = block_products([entries(first + index + k, 0, stored) for k in range(2)])
-        for k in range(2):
-            finish(index + k, pair[k])
+    group_products(first, group, entries, finish)
     for spare in range(group, out_ref.shape[0]):
         out_ref[spare] = jnp.zeros_like(out_ref[spare])
-    if group % 2:
-        face = first + group - 1
-        cut = (stored + 3) // 4 * 2
-        finish(group - 1, sum(block_products([entries(face, 0, cut), entries(face, cut, stored)])))
+    if done:
+        def missed(slot, index):
+            values, block = entry(first + index, slot)
+            out_ref[index, :times] -= 2.0 * block_products([[(values, block)]])[0]
+            return index
+
+        least = ready_ref[0, first]
+        for index in range(1, group):
+            least = jnp.minimum(least, ready_ref[0, first + index])
+
+        @pl.when(least < done)
+        def _():
+            for index in range(group):
+                lax.fori_loop(ready_ref[0, first + index], done, missed, index)
 
 
 def running_peak(sizes):
@@ -227,36 +305,45 @@
     flat = (times, faces * extent)
     block_bytes = faces * stored * extent * extent * 2
     part_bytes = group * times * extent * 4
-    robin0, robin1, half0, half1, load, stiff, record, turn, columns, partner = call(
-        prepare, [HBM] * 8,
-        (f32(*part), f32(*part), bf16(*part), bf16(*part), bf16(*flat), f32(1, faces * extent), f32(1, faces * extent),
-         s32(1, faces * extent), pltpu.SMEM((faces, 1, stored), jnp.int32), pltpu.SMEM((1, faces), jnp.int32)),
-        [pltpu.VMEM(flat, jnp.bfloat16), pltpu.VMEM(flat, jnp.bfloat16), pltpu.SemaphoreType.DMA((8,))],
-        8 * part_bytes, (VMEM,) * 8 + (SMEM,) * 2,
-    )(*(pltpu.with_memory_space_constraint(value, pltpu.HBM) for value in (
-        starting_motion[0], start_traction[0], load_response[0], stiffness, history,
-        orientation.reshape(1, -1), jnp.transpose(block_columns, (1, 0, 2)), face_partner,
-    )))
-    columns, partner = (pltpu.with_memory_space_constraint(table, pltpu.SMEM) for table in (columns, partner))
-    blocks = call(
-        fetch, [HBM], pltpu.VMEM((faces, stored, extent, extent), jnp.bfloat16),
-        [pltpu.SemaphoreType.DMA((faces,))], block_bytes,
-    )(pltpu.with_memory_space_constraint(compliance[0], pltpu.HBM))
+    in_hbm = functools.partial(pltpu.with_memory_space_constraint, memory_space=pltpu.HBM)
+    robin0, robin1, half0, half1 = call(
+        prepare, [HBM] * 2, (f32(*part), f32(*part), bf16(*part), bf16(*part)),
+        [pltpu.VMEM(flat, jnp.bfloat16), pltpu.VMEM(flat, jnp.bfloat16), pltpu.SemaphoreType.DMA((2,))],
+        8 * part_bytes,
+    )(in_hbm(starting_motion[0]), in_hbm(start_traction[0]))
+    blocks, load, stiff, record, turn, *tables = call(
+        fetch, [HBM] * 7,
+        (pltpu.VMEM((faces, stored, extent, extent), jnp.bfloat16), bf16(*flat), f32(1, faces * extent), f32(1, faces * extent),
+         s32(1, faces * extent), pltpu.SMEM((1, faces), jnp.int32), pltpu.SMEM((faces, 1, stored), jnp.int32),
+         pltpu.SMEM((faces, 1, stored), jnp.int32), pltpu.SMEM((1, faces), jnp.int32)),
+        [pltpu.SMEM((faces, 1, stored), jnp.int32), pltpu.SemaphoreType.DMA((6 + faces,))],
+        block_bytes, (VMEM,) * 5 + (SMEM,) * 4,
+    )(
+        in_hbm(compliance[0]), in_hbm(load_response[0]), in_hbm(stiffness), in_hbm(history),
+        in_hbm(orientation.reshape(1, -1)), in_hbm(jnp.transpose(block_columns, (1, 0, 2))), in_hbm(face_partner),
+    )
+    partner, *tables = (pltpu.with_memory_space_constraint(table, pltpu.SMEM) for table in tables)
 
     robin, half = [robin0, robin1], [half0, half1]
     stiffs, records = [stiff, stiff], [record, record]
     for iteration in range(ITERS):
         begin, last = iteration == 0, iteration == ITERS - 1
         other = [lax.ppermute(half[side], "row", swap) for side in range(2)]
-        ascent, mates = [None, None], [None, None]
+        ascent, mates, early = [None, None], [None, None], []
+        for side in range(0 if begin else 2):
+            early.append(call(
+                functools.partial(early_products, side), [SMEM] * 3 + [VMEM] * (3 + side) + [ANY] * side, f32(*part),
+                [pltpu.VMEM((rows * faces + 1, times, extent), jnp.bfloat16)], block_bytes,
+            )(*tables, blocks, *half, *other[:side], *early))
         for side, (axes, pairs) in enumerate((("sub", near_pairs), (("sub", "row"), far_pairs))):
+            more = (stiff, record) if begin else (early[side],)
             ascent[side] = call(
-                functools.partial(linear_section, side),
-                [SMEM] + [VMEM] * 9,
+                functools.partial(linear_section, side, begin),
+                [SMEM] * 3 + [VMEM] * (7 + len(more)),
                 f32(group + side, times + SUBLANES if begin else times, extent),
                 [pltpu.VMEM((rows * faces, times, extent), jnp.bfloat16)],
                 2 * block_bytes,
-            )(columns, blocks, *half, *other, robin[side], load, stiff, record)
+            )(*tables, blocks, *half, *other, robin[side], load, *more)
             mates[side] = lax.ppermute(ascent[side], axes, pairs)
         if last:
             return tuple(out[None] for out in call(

time: 44.5 us -> 42.8 us (0.962)
  waiting for transfers between devices: 11.5 us -> 8.43 us
  Pallas kernels: 17.8 us -> 18.9 us
    ppermute x6, waiting for transfers between devices: 7.35 us -> 4.1 us  [shards(): other = [lax.ppermute(half[side], 'row', swap) for side in range(2)]]
    pallas_call x8 -> x12, Pallas kernels: 15.7 us -> 16.8 us  [the longest x6 8.08 us: shards(): call(functools.partial(linear_section, side, begin), [SMEM] * 3 + [VMEM]...]
  transfers between devices with their start and end apart: 12 -> 12, of which waited for: 9 -> 8; matrix products, arithmetic and copies ran while one was open for 0% -> 0% of each run, Pallas kernels for 23% -> 31%
where the time goes in v4:
time: 42.8 us; the launch traced here: 42.4 us
  Pallas kernels  18.9 us (44%)
  starting transfers between devices  14.3 us (33%)
  waiting for transfers between devices  8.43 us (20%)
  between operations  0.74 us (2%)
    pallas_call x6, Pallas kernels, shards(): call(functools.partial(linear_section, side, begin), [SMEM] * 3 + [VMEM]...  8.08 us
    ppermute x6, starting transfers between devices, shards(): other = [lax.ppermute(half[side], 'row', swap) for side in range(2)]  7.56 us
    ppermute x6, starting transfers between devices, shards(): mates[side] = lax.ppermute(ascent[side], axes, pairs)  6.73 us
    pallas_call x1, Pallas kernels, shards(): call(fetch, [HBM] * 7, (pltpu.VMEM((faces, stored, extent, extent), jnp.b...  4.35 us
    ppermute x6, waiting for transfers between devices, shards(): mates[side] = lax.ppermute(ascent[side], axes, pairs)  4.33 us
    ppermute x6, waiting for transfers between devices, shards(): other = [lax.ppermute(half[side], 'row', swap) for side in range(2)]  4.1 us
    pallas_call x4, Pallas kernels, shards(): call(functools.partial(early_products, side), [SMEM] * 3 + [VMEM] * (3 +...  3.31 us
    pallas_call x1, Pallas kernels, shards(): call(local_last, [SMEM] + [VMEM] * 9, (bf16(*flat),) * 2)  1.1 us
  transfers between devices with their start and end apart: 12, of which 8 were waited for; matrix products, arithmetic and copies ran while one was open for 0% of the time, Pallas kernels for 31%

profile of v4, /device:TPU:0, one launch (start us, length us, event | category | flops | bytes accessed | tf_op | source)
XLA Modules:
  0.0 42.4 jit_solution(5215048411708280590)
XLA Ops:
  0.6 1.0 %shard_map.105 = (f32[9,32,128]{2,1,0:T(8,128)S(1)}, f32[9,32,128]{2,1,0:T(8,128)S(1)}, bf16[9,32,128]{2,1,0:T(8,128)(2,1)S(1)}, bf16[9,32,128]{2,1,0:T(8,128)(2,1)S(1)}) custom-call(bf16[32,2304]{1,0:T(8,128)(2,1)} %bitcast.9, bf16[32,2304]{1,0:T(8,128)(2,1)} %bitcast.10), custom_call_target="tpu_custom_call" | custom-call | flops 1179648 | bytes 1179648 | tf_op jit(solution)/shard_map/pallas_call | solution.py:309
  1.7 3.0 %collective-permute-start = (bf16[9,32,128]{2,1,0:T(8,128)(2,1)S(1)}, bf16[9,32,128]{2,1,0:T(8,128)(2,1)S(1)}, u32[]{:S(2)}, u32[]{:S(2)}) collective-permute-start(bf16[9,32,128]{2,1,0:T(8,128)(2,1)S(1)} %get-tuple-element.35.own0_ref), channel_id=1, source_target_pairs={{0,1},{1,0},{2,3},{3,2},{4,5},{5,4},{6,7},{7,6},{8,9},{9,8},{10,11... | collective-permute-start | bytes 221192 | tf_op jit(solution)/shard_map/ppermute | solution.py:331
  4.8 4.4 %shard_map.104 = (bf16[18,18,128,128]{3,2,1,0:T(8,128)(2,1)S(1)}, bf16[32,2304]{1,0:T(8,128)(2,1)S(1)}, f32[1,2304]{1,0:T(1,128)S(1)}, f32[1,2304]{1,0:T(1,128)S...) custom-call(bf16[18,18,128,128]{3,2,1,0:T(8,128)(2,1)} %bitcast.8, ...), custom_call_target="tpu_custom_call" | custom-call | flops 10616832 | bytes 10616832 | tf_op jit(solution)/shard_map/pallas_call | solution.py:314
  9.1 1.8 %shard_map.108.own_ref = f32[10,40,128]{2,1,0:T(8,128)S(1)} custom-call(s32[18,1,18]{2,1,0:T(1,128)S(4)} %get-tuple-element.31.order_ref, s32[18,1,18]{2,1,0:T(1,128)S(4)} %get-tuple-element.32.sorted_ref, s32[1,18]{1,0:T(1,128)S(4)} %get-tuple-element.33.ready_ref, bf16[18,18,128,128]{3,2,1,0:T(8,128)(2,1)S(1)} %get-tuple-element.34.compliance_ref, ...), custom_call_target="tpu_custom_call" | custom-call | flops 21233664 | bytes 21233664 | tf_op jit(solution)/shard_map/pallas_call | solution.py:340
  10.9 2.0 %collective-permute-start.3 = (f32[10,40,128]{2,1,0:T(8,128)S(1)}, f32[10,40,128]{2,1,0:T(8,128)S(1)}, u32[]{:S(2)}, u32[]{:S(2)}) collective-permute-start(f32[10,40,128]{2,1,0:T(8,128)S(1)} %shard_map.108.own_ref), channel_id=1, source_target_pairs={{0,1},{1,0},{2,4},{3,5},{4,2},{5,3},{6,8},{7,9},{8,6},{9,7},{10,12... | collective-permute-start | bytes 614408 | tf_op jit(solution)/shard_map/ppermute | solution.py:347
  12.9 1.8 %shard_map.106.own_ref = f32[9,40,128]{2,1,0:T(8,128)S(1)} custom-call(s32[18,1,18]{2,1,0:T(1,128)S(4)} %get-tuple-element.31.order_ref, s32[18,1,18]{2,1,0:T(1,128)S(4)} %get-tuple-element.32.sorted_ref, s32[1,18]{1,0:T(1,128)S(4)} %get-tuple-element.33.ready_ref, bf16[18,18,128,128]{3,2,1,0:T(8,128)(2,1)S(1)} %get-tuple-element.34.compliance_ref, ...), custom_call_target="tpu_custom_call" | custom-call | flops 21233664 | bytes 21233664 | tf_op jit(solution)/shard_map/pallas_call | solution.py:340
  14.9 1.3 %collective-permute-done.2.mate_ref = f32[9,40,128]{2,1,0:T(8,128)S(1)} collective-permute-done((f32[9,40,128]{2,1,0:T(8,128)S(1)}, f32[9,40,128]{2,1,0:T(8,128)S(1)}, u32[]{:S(2)}, u32[]{:S(2)}) %collective-permute-start.2) | collective-permute-done | bytes 184352 | tf_op jit(solution)/shard_map/ppermute | solution.py:347
  16.4 1.3 %collective-permute-start.4 = (bf16[9,32,128]{2,1,0:T(8,128)(2,1)S(1)}, bf16[9,32,128]{2,1,0:T(8,128)(2,1)S(1)}, u32[]{:S(2)}, u32[]{:S(2)}) collective-permute-start(bf16[9,32,128]{2,1,0:T(8,128)(2,1)S(1)} %get-tuple-element.41.own0_ref), channel_id=1, source_target_pairs={{0,1},{1,0},{2,3},{3,2},{4,5},{5,4},{6,7},{7,6},{8,9},{9,8},{10,11... | collective-permute-start | bytes 221192 | tf_op jit(solution)/shard_map/ppermute | solution.py:331
  17.8 0.3 shard_map.109
  18.1 1.0 %collective-permute-start.5 = (bf16[9,32,128]{2,1,0:T(8,128)(2,1)S(1)}, bf16[9,32,128]{2,1,0:T(8,128)(2,1)S(1)}, u32[]{:S(2)}, u32[]{:S(2)}) collective-permute-start(bf16[9,32,128]{2,1,0:T(8,128)(2,1)S(1)} %get-tuple-element.43.own1_ref), channel_id=1, source_target_pairs={{0,1},{1,0},{2,3},{3,2},{4,5},{5,4},{6,7},{7,6},{8,9},{9,8},{10,11... | collective-permute-start | bytes 221192 | tf_op jit(solution)/shard_map/ppermute | solution.py:331
  19.0 0.7 %shard_map.110.refs_0_.refs_1_ = f32[9,32,128]{2,1,0:T(8,128)S(1)} custom-call(s32[18,1,18]{2,1,0:T(1,128)S(4)} %get-tuple-element.31.order_ref, s32[18,1,18]{2,1,0:T(1,128)S(4)} %get-tuple-element.32.sorted_ref, s32[1,18]{1,0:T(1,128)S(4)} %get-tuple-element.33.ready_ref, bf16[18,18,128,128]{3,2,1,0:T(8,128)(2,1)S(1)} %get-tuple-element.34.compliance_ref, ...), custom_call_target="tpu_custom_call" | custom-call | flops 10616832 | bytes 10616832 | tf_op jit(solution)/shard_map/pallas_call | solution.py:334
  19.7 1.2 %collective-permute-done.4.other0_ref.refs_0_ = bf16[9,32,128]{2,1,0:T(8,128)(2,1)S(1)} collective-permute-done((bf16[9,32,128]{2,1,0:T(8,128)(2,1)S(1)}, bf16[9,32,128]{2,1,0:T(8,128)(2,1)S(1)}, u32[]{:S(2)}, u32[]{:S(2)}) %collective-permute-start.4) | collective-permute-done | bytes 73760 | tf_op jit(solution)/shard_map/ppermute | solution.py:331
  20.9 1.0 %shard_map.113.refs_0_ = f32[9,32,128]{2,1,0:T(8,128)S(1)} custom-call(s32[18,1,18]{2,1,0:T(1,128)S(4)} %get-tuple-element.31.order_ref, s32[18,1,18]{2,1,0:T(1,128)S(4)} %get-tuple-element.32.sorted_ref, s32[1,18]{1,0:T(1,128)S(4)} %get-tuple-element.33.ready_ref, bf16[18,18,128,128]{3,2,1,0:T(8,128)(2,1)S(1)} %get-tuple-element.34.compliance_ref, ...), custom_call_target="tpu_custom_call" | custom-call | flops 10616832 | bytes 10616832 | tf_op jit(solution)/shard_map/pallas_call | solution.py:334
  21.9 0.6 %collective-permute-done.5.other1_ref = bf16[9,32,128]{2,1,0:T(8,128)(2,1)S(1)} collective-permute-done((bf16[9,32,128]{2,1,0:T(8,128)(2,1)S(1)}, bf16[9,32,128]{2,1,0:T(8,128)(2,1)S(1)}, u32[]{:S(2)}, u32[]{:S(2)}) %collective-permute-start.5) | collective-permute-done | bytes 73760 | tf_op jit(solution)/shard_map/ppermute | solution.py:331
  22.5 0.9 %shard_map.114.own_ref = f32[10,32,128]{2,1,0:T(8,128)S(1)} custom-call(s32[18,1,18]{2,1,0:T(1,128)S(4)} %get-tuple-element.31.order_ref, s32[18,1,18]{2,1,0:T(1,128)S(4)} %get-tuple-element.32.sorted_ref, s32[1,18]{1,0:T(1,128)S(4)} %get-tuple-element.33.ready_ref, bf16[18,18,128,128]{3,2,1,0:T(8,128)(2,1)S(1)} %get-tuple-element.34.compliance_ref, ...), custom_call_target="tpu_custom_call" | custom-call | flops 21233664 | bytes 21233664 | tf_op jit(solution)/shard_map/pallas_call | solution.py:340
  23.3 1.6 %collective-permute-start.7 = (f32[10,32,128]{2,1,0:T(8,128)S(1)}, f32[10,32,128]{2,1,0:T(8,128)S(1)}, u32[]{:S(2)}, u32[]{:S(2)}) collective-permute-start(f32[10,32,128]{2,1,0:T(8,128)S(1)} %shard_map.114.own_ref), channel_id=1, source_target_pairs={{0,1},{1,0},{2,4},{3,5},{4,2},{5,3},{6,8},{7,9},{8,6},{9,7},{10,12... | collective-permute-start | bytes 491528 | tf_op jit(solution)/shard_map/ppermute | solution.py:347
  24.9 1.4 %shard_map.111.own_ref = f32[9,32,128]{2,1,0:T(8,128)S(1)} custom-call(s32[18,1,18]{2,1,0:T(1,128)S(4)} %get-tuple-element.31.order_ref, s32[18,1,18]{2,1,0:T(1,128)S(4)} %get-tuple-element.32.sorted_ref, s32[1,18]{1,0:T(1,128)S(4)} %get-tuple-element.33.ready_ref, bf16[18,18,128,128]{3,2,1,0:T(8,128)(2,1)S(1)} %get-tuple-element.34.compliance_ref, ...), custom_call_target="tpu_custom_call" | custom-call | flops 21233664 | bytes 21233664 | tf_op jit(solution)/shard_map/pallas_call | solution.py:340
  26.3 1.0 %collective-permute-start.6 = (f32[9,32,128]{2,1,0:T(8,128)S(1)}, f32[9,32,128]{2,1,0:T(8,128)S(1)}, u32[]{:S(2)}, u32[]{:S(2)}) collective-permute-start(f32[9,32,128]{2,1,0:T(8,128)S(1)} %shard_map.111.own_ref), channel_id=1, source_target_pairs={{0,2},{2,0},{4,6},{6,4},{8,10},{10,8},{12,14},{14,12},{16,18},{18,... | collective-permute-start | bytes 442376 | tf_op jit(solution)/shard_map/ppermute | solution.py:347
  27.3 1.0 %collective-permute-done.6.mate_ref = f32[9,32,128]{2,1,0:T(8,128)S(1)} collective-permute-done((f32[9,32,128]{2,1,0:T(8,128)S(1)}, f32[9,32,128]{2,1,0:T(8,128)S(1)}, u32[]{:S(2)}, u32[]{:S(2)}) %collective-permute-start.6) | collective-permute-done | bytes 147488 | tf_op jit(solution)/shard_map/ppermute | solution.py:347
  28.6 1.7 %collective-permute-start.8 = (bf16[9,32,128]{2,1,0:T(8,128)(2,1)S(1)}, bf16[9,32,128]{2,1,0:T(8,128)(2,1)S(1)}, u32[]{:S(2)}, u32[]{:S(2)}) collective-permute-start(bf16[9,32,128]{2,1,0:T(8,128)(2,1)S(1)} %get-tuple-element.47.own0_ref), channel_id=1, source_target_pairs={{0,1},{1,0},{2,3},{3,2},{4,5},{5,4},{6,7},{7,6},{8,9},{9,8},{10,11... | collective-permute-start | bytes 221192 | tf_op jit(solution)/shard_map/ppermute | solution.py:331
  30.6 0.4 %collective-permute-start.9 = (bf16[9,32,128]{2,1,0:T(8,128)(2,1)S(1)}, bf16[9,32,128]{2,1,0:T(8,128)(2,1)S(1)}, u32[]{:S(2)}, u32[]{:S(2)}) collective-permute-start(bf16[9,32,128]{2,1,0:T(8,128)(2,1)S(1)} %get-tuple-element.51.own1_ref), channel_id=1, source_target_pairs={{0,1},{1,0},{2,3},{3,2},{4,5},{5,4},{6,7},{7,6},{8,9},{9,8},{10,11... | collective-permute-start | bytes 221192 | tf_op jit(solution)/shard_map/ppermute | solution.py:331
  31.0 0.7 %shard_map.116.refs_0_.refs_1_ = f32[9,32,128]{2,1,0:T(8,128)S(1)} custom-call(s32[18,1,18]{2,1,0:T(1,128)S(4)} %get-tuple-element.31.order_ref, s32[18,1,18]{2,1,0:T(1,128)S(4)} %get-tuple-element.32.sorted_ref, s32[1,18]{1,0:T(1,128)S(4)} %get-tuple-element.33.ready_ref, bf16[18,18,128,128]{3,2,1,0:T(8,128)(2,1)S(1)} %get-tuple-element.34.compliance_ref, ...), custom_call_target="tpu_custom_call" | custom-call | flops 10616832 | bytes 10616832 | tf_op jit(solution)/shard_map/pallas_call | solution.py:334
  31.7 1.5 %collective-permute-done.8.other0_ref.refs_0_ = bf16[9,32,128]{2,1,0:T(8,128)(2,1)S(1)} collective-permute-done((bf16[9,32,128]{2,1,0:T(8,128)(2,1)S(1)}, bf16[9,32,128]{2,1,0:T(8,128)(2,1)S(1)}, u32[]{:S(2)}, u32[]{:S(2)}) %collective-permute-start.8) | collective-permute-done | bytes 73760 | tf_op jit(solution)/shard_map/ppermute | solution.py:331
  33.2 1.0 %shard_map.118.refs_0_ = f32[9,32,128]{2,1,0:T(8,128)S(1)} custom-call(s32[18,1,18]{2,1,0:T(1,128)S(4)} %get-tuple-element.31.order_ref, s32[18,1,18]{2,1,0:T(1,128)S(4)} %get-tuple-element.32.sorted_ref, s32[1,18]{1,0:T(1,128)S(4)} %get-tuple-element.33.ready_ref, bf16[18,18,128,128]{3,2,1,0:T(8,128)(2,1)S(1)} %get-tuple-element.34.compliance_ref, ...), custom_call_target="tpu_custom_call" | custom-call | flops 10616832 | bytes 10616832 | tf_op jit(solution)/shard_map/pallas_call | solution.py:334
  34.2 0.8 %collective-permute-done.9.other1_ref = bf16[9,32,128]{2,1,0:T(8,128)(2,1)S(1)} collective-permute-done((bf16[9,32,128]{2,1,0:T(8,128)(2,1)S(1)}, bf16[9,32,128]{2,1,0:T(8,128)(2,1)S(1)}, u32[]{:S(2)}, u32[]{:S(2)}) %collective-permute-start.9) | collective-permute-done | bytes 73760 | tf_op jit(solution)/shard_map/ppermute | solution.py:331
  35.0 0.9 %shard_map.119.own1_ref = f32[10,32,128]{2,1,0:T(8,128)S(1)} custom-call(s32[18,1,18]{2,1,0:T(1,128)S(4)} %get-tuple-element.31.order_ref, s32[18,1,18]{2,1,0:T(1,128)S(4)} %get-tuple-element.32.sorted_ref, s32[1,18]{1,0:T(1,128)S(4)} %get-tuple-element.33.ready_ref, bf16[18,18,128,128]{3,2,1,0:T(8,128)(2,1)S(1)} %get-tuple-element.34.compliance_ref, ...), custom_call_target="tpu_custom_call" | custom-call | flops 21233664 | bytes 21233664 | tf_op jit(solution)/shard_map/pallas_call | solution.py:340
  35.9 1.5 %collective-permute-start.11 = (f32[10,32,128]{2,1,0:T(8,128)S(1)}, f32[10,32,128]{2,1,0:T(8,128)S(1)}, u32[]{:S(2)}, u32[]{:S(2)}) collective-permute-start(f32[10,32,128]{2,1,0:T(8,128)S(1)} %shard_map.119.own1_ref), channel_id=1, source_target_pairs={{0,1},{1,0},{2,4},{3,5},{4,2},{5,3},{6,8},{7,9},{8,6},{9,7},{10,12... | collective-permute-start | bytes 491528 | tf_op jit(solution)/shard_map/ppermute | solution.py:347
  37.4 1.4 %shard_map.117.own0_ref = f32[9,32,128]{2,1,0:T(8,128)S(1)} custom-call(s32[18,1,18]{2,1,0:T(1,128)S(4)} %get-tuple-element.31.order_ref, s32[18,1,18]{2,1,0:T(1,128)S(4)} %get-tuple-element.32.sorted_ref, s32[1,18]{1,0:T(1,128)S(4)} %get-tuple-element.33.ready_ref, bf16[18,18,128,128]{3,2,1,0:T(8,128)(2,1)S(1)} %get-tuple-element.34.compliance_ref, ...), custom_call_target="tpu_custom_call" | custom-call | flops 21233664 | bytes 21233664 | tf_op jit(solution)/shard_map/pallas_call | solution.py:340
  38.8 0.4 collective-permute-start.10
  39.2 1.0 %collective-permute-done.10.mate0_ref = f32[9,32,128]{2,1,0:T(8,128)S(1)} collective-permute-done((f32[9,32,128]{2,1,0:T(8,128)S(1)}, f32[9,32,128]{2,1,0:T(8,128)S(1)}, u32[]{:S(2)}, u32[]{:S(2)}) %collective-permute-start.10) | collective-permute-done | bytes 147488 | tf_op jit(solution)/shard_map/ppermute | solution.py:347
  40.2 1.0 %collective-permute-done.11.mate1_ref = f32[10,32,128]{2,1,0:T(8,128)S(1)} collective-permute-done((f32[10,32,128]{2,1,0:T(8,128)S(1)}, f32[10,32,128]{2,1,0:T(8,128)S(1)}, u32[]{:S(2)}, u32[]{:S(2)}) %collective-permute-start.11) | collective-permute-done | bytes 163872 | tf_op jit(solution)/shard_map/ppermute | solution.py:347
  41.3 1.1 %shard_map.120 = (bf16[32,2304]{1,0:T(8,128)(2,1)}, bf16[32,2304]{1,0:T(8,128)(2,1)}) custom-call(s32[1,18]{1,0:T(1,128)S(4)} %get-tuple-element.29.partner_ref, s32[1,2304]{1,0:T(1,128)S(1)} %get-tuple-element.30.turn_ref, f32[9,32,128]{2,1,0:T(8,128)S(1)} %shard_map.117.own0_ref, f32[10,32,128]{2,1,0:T(8,128)S(1)} %shard_map.119.own1_ref, ...), custom_call_target="tpu_custom_call" | custom-call | tf_op jit(solution)/shard_map/pallas_call | solution.py:349
  (9 shorter events, 1.1 us)
Async XLA Ops:
  1.7 7.4 %collective-permute-start = (bf16[9,32,128]{2,1,0:T(8,128)(2,1)S(1)}, bf16[9,32,128]{2,1,0:T(8,128)(2,1)S(1)}, u32[]{:S(2)}, u32[]{:S(2)}) collective-permute-start(bf16[9,32,128]{2,1,0:T(8,128)(2,1)S(1)} %get-tuple-element.35.own0_ref), channel_id=1, source_target_pairs={{0,1},{1,0},{2,3},{3,2},{4,5},{5,4},{6,7},{7,6},{8,9},{9,8},{10,11... | collective-permute-start | bytes 221192 | tf_op jit(solution)/shard_map/ppermute | solution.py:331
  4.7 4.5 %collective-permute-start.1 = (bf16[9,32,128]{2,1,0:T(8,128)(2,1)S(1)}, bf16[9,32,128]{2,1,0:T(8,128)(2,1)S(1)}, u32[]{:S(2)}, u32[]{:S(2)}) collective-permute-start(bf16[9,32,128]{2,1,0:T(8,128)(2,1)S(1)} %get-tuple-element.36.own1_ref), channel_id=1, source_target_pairs={{0,1},{1,0},{2,3},{3,2},{4,5},{5,4},{6,7},{7,6},{8,9},{9,8},{10,11... | collective-permute-start | bytes 221192 | tf_op jit(solution)/shard_map/ppermute | solution.py:331
  10.9 6.9 %collective-permute-start.3 = (f32[10,40,128]{2,1,0:T(8,128)S(1)}, f32[10,40,128]{2,1,0:T(8,128)S(1)}, u32[]{:S(2)}, u32[]{:S(2)}) collective-permute-start(f32[10,40,128]{2,1,0:T(8,128)S(1)} %shard_map.108.own_ref), channel_id=1, source_target_pairs={{0,1},{1,0},{2,4},{3,5},{4,2},{5,3},{6,8},{7,9},{8,6},{9,7},{10,12... | collective-permute-start | bytes 614408 | tf_op jit(solution)/shard_map/ppermute | solution.py:347
  14.7 1.5 %collective-permute-start.2 = (f32[9,40,128]{2,1,0:T(8,128)S(1)}, f32[9,40,128]{2,1,0:T(8,128)S(1)}, u32[]{:S(2)}, u32[]{:S(2)}) collective-permute-start(f32[9,40,128]{2,1,0:T(8,128)S(1)} %shard_map.106.own_ref), channel_id=1, source_target_pairs={{0,2},{2,0},{4,6},{6,4},{8,10},{10,8},{12,14},{14,12},{16,18},{18,... | collective-permute-start | bytes 552968 | tf_op jit(solution)/shard_map/ppermute | solution.py:347
  16.4 4.4 %collective-permute-start.4 = (bf16[9,32,128]{2,1,0:T(8,128)(2,1)S(1)}, bf16[9,32,128]{2,1,0:T(8,128)(2,1)S(1)}, u32[]{:S(2)}, u32[]{:S(2)}) collective-permute-start(bf16[9,32,128]{2,1,0:T(8,128)(2,1)S(1)} %get-tuple-element.41.own0_ref), channel_id=1, source_target_pairs={{0,1},{1,0},{2,3},{3,2},{4,5},{5,4},{6,7},{7,6},{8,9},{9,8},{10,11... | collective-permute-start | bytes 221192 | tf_op jit(solution)/shard_map/ppermute | solution.py:331
  18.1 4.4 %collective-permute-start.5 = (bf16[9,32,128]{2,1,0:T(8,128)(2,1)S(1)}, bf16[9,32,128]{2,1,0:T(8,128)(2,1)S(1)}, u32[]{:S(2)}, u32[]{:S(2)}) collective-permute-start(bf16[9,32,128]{2,1,0:T(8,128)(2,1)S(1)} %get-tuple-element.43.own1_ref), channel_id=1, source_target_pairs={{0,1},{1,0},{2,3},{3,2},{4,5},{5,4},{6,7},{7,6},{8,9},{9,8},{10,11... | collective-permute-start | bytes 221192 | tf_op jit(solution)/shard_map/ppermute | solution.py:331
  23.3 7.0 %collective-permute-start.7 = (f32[10,32,128]{2,1,0:T(8,128)S(1)}, f32[10,32,128]{2,1,0:T(8,128)S(1)}, u32[]{:S(2)}, u32[]{:S(2)}) collective-permute-start(f32[10,32,128]{2,1,0:T(8,128)S(1)} %shard_map.114.own_ref), channel_id=1, source_target_pairs={{0,1},{1,0},{2,4},{3,5},{4,2},{5,3},{6,8},{7,9},{8,6},{9,7},{10,12... | collective-permute-start | bytes 491528 | tf_op jit(solution)/shard_map/ppermute | solution.py:347
  26.3 2.0 %collective-permute-start.6 = (f32[9,32,128]{2,1,0:T(8,128)S(1)}, f32[9,32,128]{2,1,0:T(8,128)S(1)}, u32[]{:S(2)}, u32[]{:S(2)}) collective-permute-start(f32[9,32,128]{2,1,0:T(8,128)S(1)} %shard_map.111.own_ref), channel_id=1, source_target_pairs={{0,2},{2,0},{4,6},{6,4},{8,10},{10,8},{12,14},{14,12},{16,18},{18,... | collective-permute-start | bytes 442376 | tf_op jit(solution)/shard_map/ppermute | solution.py:347
  28.6 4.6 %collective-permute-start.8 = (bf16[9,32,128]{2,1,0:T(8,128)(2,1)S(1)}, bf16[9,32,128]{2,1,0:T(8,128)(2,1)S(1)}, u32[]{:S(2)}, u32[]{:S(2)}) collective-permute-start(bf16[9,32,128]{2,1,0:T(8,128)(2,1)S(1)} %get-tuple-element.47.own0_ref), channel_id=1, source_target_pairs={{0,1},{1,0},{2,3},{3,2},{4,5},{5,4},{6,7},{7,6},{8,9},{9,8},{10,11... | collective-permute-start | bytes 221192 | tf_op jit(solution)/shard_map/ppermute | solution.py:331
  30.6 4.4 %collective-permute-start.9 = (bf16[9,32,128]{2,1,0:T(8,128)(2,1)S(1)}, bf16[9,32,128]{2,1,0:T(8,128)(2,1)S(1)}, u32[]{:S(2)}, u32[]{:S(2)}) collective-permute-start(bf16[9,32,128]{2,1,0:T(8,128)(2,1)S(1)} %get-tuple-element.51.own1_ref), channel_id=1, source_target_pairs={{0,1},{1,0},{2,3},{3,2},{4,5},{5,4},{6,7},{7,6},{8,9},{9,8},{10,11... | collective-permute-start | bytes 221192 | tf_op jit(solution)/shard_map/ppermute | solution.py:331
  35.9 5.4 %collective-permute-start.11 = (f32[10,32,128]{2,1,0:T(8,128)S(1)}, f32[10,32,128]{2,1,0:T(8,128)S(1)}, u32[]{:S(2)}, u32[]{:S(2)}) collective-permute-start(f32[10,32,128]{2,1,0:T(8,128)S(1)} %shard_map.119.own1_ref), channel_id=1, source_target_pairs={{0,1},{1,0},{2,4},{3,5},{4,2},{5,3},{6,8},{7,9},{8,6},{9,7},{10,12... | collective-permute-start | bytes 491528 | tf_op jit(solution)/shard_map/ppermute | solution.py:347
  38.8 1.4 %collective-permute-start.10 = (f32[9,32,128]{2,1,0:T(8,128)S(1)}, f32[9,32,128]{2,1,0:T(8,128)S(1)}, u32[]{:S(2)}, u32[]{:S(2)}) collective-permute-start(f32[9,32,128]{2,1,0:T(8,128)S(1)} %shard_map.117.own0_ref), channel_id=1, source_target_pairs={{0,2},{2,0},{4,6},{6,4},{8,10},{10,8},{12,14},{14,12},{16,18},{18,... | collective-permute-start | bytes 442376 | tf_op jit(solution)/shard_map/ppermute | solution.py:347
